TPU v7x, 128 devices: a whole 4x4x4 slice. The times are simulated.
128 devices in a mesh: mlong: 16 (over z_lo, y, core), mshort: 8 (over z_hi, x).
Axes of the slice: x: 4, y: 4, z: 4 (z_hi: 2, z_lo: 2; z = z_hi * 2 + z_lo), core: 2. Of those that a mesh axis runs over, the one named last changes fastest.
Arguments:
- acq_traces: bfloat16 [65536, 1024], P(('mlong', 'mshort')), may hold values from -6 to 6
- route_owner: int32 [65536], P(('mlong', 'mshort')), may hold values from -1 to 127, as said below
- route_row: int32 [65536], P(('mlong', 'mshort')), may hold values from -1 to 511, as said below
- route_fold: int32 [65536], P(('mlong', 'mshort')), may hold values from 0 to 3
- sample_bits: int32 [65536, 64], P(('mlong', 'mshort')), may hold values from 0 to 65535
- left_factors: bfloat16 [65536, 4, 128], P(('mlong', 'mshort')), may hold values from -0.5 to 0.5
- right_factors: bfloat16 [4, 131072, 128], P(None, ('mlong', 'mshort')), may hold values from -6 to 6
Outputs:
- new_right: float32 [4, 131072, 128], P(None, ('mlong', 'mshort'))
- trace_residuals: bfloat16 [65536, 1024], P(('mlong', 'mshort'))
Inputs may be any that keep to these rules, and one draw needn't show every extreme that they name: route_owner: -1 marks an empty slot. In each device's 16 * 32 slots no owner is named more than 4 times; some owner is named exactly 4 times in every device's slots. Every owner is named somewhere. route_row: -1 exactly where route_owner is -1. No pair (route_owner, route_row) occurs twice.
All inputs are finite; a program needn't handle non-finite values.
Results may differ from a plain program's by a relative error of at most 0.0036.
Values may be sent and summed in bfloat16 or wider, within the bound.
No kernel may reach another device: no remote copies, remote signals or barrier semaphores. Data moves between devices by JAX's collectives and lax.ppermute only.
A program may use at most 64 MiB of HBM per device.

v0:
```python
import jax
import jax.numpy as jnp
from jax import lax
from jax.experimental import pallas as pl
from jax.experimental.pallas import tpu as pltpu
from jax.sharding import PartitionSpec as P

RANK = 128
FOLDS = 4
H = 4
CX = 16
CY = 32
W = 1024
ROWS = CX * CY
HALF = W // 2
LANE = 128
CAP = 4
SLOT = 2 * CAP
NSLOT = 128 * SLOT
EXT = W + LANE
LEXT = FOLDS * RANK + LANE
STRIP = H * CY
SIDE = H * CX
TALL = H * (CX + 2 * H)
HALO = 2 * STRIP + 2 * TALL
PANEL = 16

BF = jnp.bfloat16
F32 = jnp.float32
AXES = ("mlong", "mshort")


def _iota(shape, dim):
    return lax.broadcasted_iota(jnp.int32, shape, dim)


def _hot(cond):
    return jnp.where(cond, 1.0, 0.0).astype(BF)


def _dot(a, b):
    return jnp.dot(a, b, preferred_element_type=F32)


def _dot_nt(a, b):
    return lax.dot_general(a, b, (((1,), (1,)), ((), ())), preferred_element_type=F32)


def _params(limit=32):
    return pltpu.CompilerParams(vmem_limit_bytes=limit * 1024 * 1024)


def _cost(flops, nbytes):
    return pl.CostEstimate(flops=flops, bytes_accessed=nbytes, transcendentals=0)


def _side_select(shape, first):
    r = _iota(shape, 0)
    m = _iota(shape, 1)
    return _hot(m == (r // H) * CY + first + r % H)


def _route_body(own_ref, row_ref, fold_ref, tr_ref, send_ref, place_ref):
    own = own_ref[...]
    row = row_ref[...]
    valid = own >= 0
    ownf = own.astype(F32)
    sub = _iota((LANE, ROWS), 0)
    flag = jnp.where(valid, 1.0, 0.0)
    meta = jnp.where(sub == 0, flag, 0.0)
    meta = jnp.where(sub == 1, (row >> 5).astype(F32), meta)
    meta = jnp.where(sub == 2, (row & 31).astype(F32), meta)
    meta = jnp.where(sub == 3, (fold_ref[...] + 1).astype(F32), meta)
    meta = jnp.where(sub == 4, ownf, meta)
    meta_t = meta.T
    ocol = meta_t[:, 4:5]
    same = ocol == ownf
    rs = _iota((ROWS, ROWS), 0)
    cs = _iota((ROWS, ROWS), 1)
    within = jnp.sum(jnp.where(same & (rs < cs), 1.0, 0.0), axis=0, keepdims=True)
    place = jnp.where(valid, ownf * SLOT + within, -64.0).astype(jnp.int32)
    within_c = jnp.sum(jnp.where(same & (cs < rs), 1.0, 0.0), axis=1, keepdims=True)
    place_c = jnp.where(ocol >= 0.0, ocol * SLOT + within_c, -64.0)
    place_ref[...] = jnp.broadcast_to(place_c, (ROWS, LANE)).astype(jnp.int32)
    meta_b = meta_t.astype(BF)
    step = 256
    for base in range(0, NSLOT, step):
        r = _iota((step, ROWS), 0) + base
        hot0 = _hot(r == place)
        hot1 = _hot(r == place + CAP)
        y = _dot(hot0, tr_ref[:, :HALF]) + _dot(hot1, tr_ref[:, HALF:])
        send_ref[base : base + step, :HALF] = y.astype(BF)
        send_ref[base : base + step, HALF:] = _dot(hot0 + hot1, meta_b).astype(BF)


def _route(own, row, fold, traces):
    return pl.pallas_call(
        _route_body,
        out_shape=(
            jax.ShapeDtypeStruct((NSLOT, HALF + LANE), BF),
            jax.ShapeDtypeStruct((ROWS, LANE), jnp.int32),
        ),
        compiler_params=_params(60),
        cost_estimate=_cost(10**9, 4 * 10**6),
        name="route",
    )(own, row, fold, traces)


def _slot_rows(meta):
    return jnp.where(meta[0] > 0.5, meta[1] * CY + meta[2], -1.0).astype(jnp.int32)


def _place_body(got_ref, core_ref, top_ref, bot_ref, left_ref, right_ref):
    meta = got_ref[:, HALF:].astype(F32).T
    m = _slot_rows((meta[0:1], meta[1:2], meta[2:3]))
    half = (_iota((1, NSLOT), 1) // CAP) % 2
    m0 = jnp.where(half == 0, m, -1)
    m1 = jnp.where(half == 1, m, -1)
    step = 128
    for base in range(0, ROWS, step):
        r = _iota((step, NSLOT), 0) + base
        hot0 = _hot(r == m0)
        hot1 = _hot(r == m1)
        d0 = _dot(hot0, got_ref[:, :HALF]).astype(BF)
        d1 = _dot(hot1, got_ref[:, :HALF]).astype(BF)
        f = _dot(hot0, got_ref[:, HALF:])[:, 3:4]
        f = jnp.broadcast_to(f, (step, LANE)).astype(BF)
        spots = [(core_ref, base)]
        if base == 0:
            spots.append((top_ref, 0))
        if base == ROWS - STRIP:
            spots.append((bot_ref, 0))
        for ref, at in spots:
            ref[at : at + step, :HALF] = d0
            ref[at : at + step, HALF:W] = d1
            ref[at : at + step, W:] = f
    core = core_ref[...]
    left_ref[...] = _dot(_side_select((SIDE, ROWS), 0), core).astype(BF)
    right_ref[...] = _dot(_side_select((SIDE, ROWS), CY - H), core).astype(BF)


def _place(got):
    return pl.pallas_call(
        _place_body,
        out_shape=(
            jax.ShapeDtypeStruct((ROWS, EXT), BF),
            jax.ShapeDtypeStruct((STRIP, EXT), BF),
            jax.ShapeDtypeStruct((STRIP, EXT), BF),
            jax.ShapeDtypeStruct((SIDE, EXT), BF),
            jax.ShapeDtypeStruct((SIDE, EXT), BF),
        ),
        compiler_params=_params(),
        cost_estimate=_cost(10**9, 4 * 10**6),
        name="to_grid",
    )(got)


def _pack_body(up_ref, down_ref, left_ref, right_ref, to_left_ref, to_right_ref):
    for first, side, out in ((0, left_ref, to_left_ref), (CY - H, right_ref, to_right_ref)):
        pick = _side_select((H * H, STRIP), first)
        out[: H * H, :] = _dot(pick, up_ref[...]).astype(BF)
        out[H * H : H * H + SIDE, :] = side[...]
        out[H * H + SIDE :, :] = _dot(pick, down_ref[...]).astype(BF)


def _pack(up, down, left, right, name):
    width = up.shape[1]
    return pl.pallas_call(
        _pack_body,
        out_shape=(
            jax.ShapeDtypeStruct((TALL, width), BF),
            jax.ShapeDtypeStruct((TALL, width), BF),
        ),
        compiler_params=_params(),
        cost_estimate=_cost(10**7, 10**6),
        name=name,
    )(up, down, left, right)


def _along(to_up, to_down, axis):
    fwd = [(i, i + 1) for i in range(lax.axis_size(axis) - 1)]
    before = lax.ppermute(to_down, axis, fwd)
    after = lax.ppermute(to_up, axis, [(j, i) for i, j in fwd])
    return before, after


def _lext_body(left_ref, bits_ref, core_ref, top_ref, bot_ref, lside_ref, rside_ref):
    core_ref[:, : FOLDS * RANK] = left_ref[...]
    bits = bits_ref[...]
    low = (bits & 255).astype(F32)
    high = (bits >> 8).astype(F32)
    core_ref[:, FOLDS * RANK :] = jnp.concatenate([low, high], axis=1).astype(BF)
    core = core_ref[...]
    top_ref[...] = core[:STRIP]
    bot_ref[...] = core[ROWS - STRIP :]
    lside_ref[...] = _dot(_side_select((SIDE, ROWS), 0), core).astype(BF)
    rside_ref[...] = _dot(_side_select((SIDE, ROWS), CY - H), core).astype(BF)


def _lext(left, bits):
    return pl.pallas_call(
        _lext_body,
        out_shape=(
            jax.ShapeDtypeStruct((ROWS, LEXT), BF),
            jax.ShapeDtypeStruct((STRIP, LEXT), BF),
            jax.ShapeDtypeStruct((STRIP, LEXT), BF),
            jax.ShapeDtypeStruct((SIDE, LEXT), BF),
            jax.ShapeDtypeStruct((SIDE, LEXT), BF),
        ),
        compiler_params=_params(),
        cost_estimate=_cost(10**8, 2 * 10**6),
        name="left_rows",
    )(left, bits)


def _recip(x):
    r = pl.reciprocal(x, approx=True)
    r = r * (2.0 - x * r)
    return r * (2.0 - x * r)


def _split3(x):
    hi = x.astype(BF)
    rest = x - hi.astype(F32)
    mid = rest.astype(BF)
    return hi, mid, (rest - mid.astype(F32)).astype(BF)


def _outer6(a, b):
    ah, am, al = _split3(a)
    bh, bm, bl = _split3(b)
    left = jnp.concatenate([ah, ah, am, ah, am, al], axis=0)
    right = jnp.concatenate([bh, bm, bh, bl, bm, bh], axis=0)
    return lax.dot_general(left, right, (((0,), (0,)), ((), ())), preferred_element_type=F32)


def _eliminate(g_ref, first, last):
    lane = _iota((FOLDS, PANEL, RANK), 2)
    sub = _iota((FOLDS, PANEL, RANK), 1)
    lane8 = _iota((FOLDS, 8, RANK), 2)
    lane_all = _iota((RANK, RANK), 1)
    rep = lambda a, n: jnp.broadcast_to(a, (FOLDS, n, RANK))
    tall = lambda a: jnp.concatenate([a] * (PANEL // 8), axis=1)
    for lo in range(first, last, PANEL):
        start = g_ref[:, lo : lo + PANEL, :]
        x = start
        for k in range(0, PANEL, 4):
            c = lo + k
            c0, c1, c2, c3 = (rep(x[:, :, c + j : c + j + 1], PANEL) for j in range(4))
            group8 = (lane8 >= c) & (lane8 < c + 4)
            r0, r1, r2, r3 = (
                jnp.where(group8, jnp.where(lane8 == c + i, 1.0, 0.0), rep(x[:, k + i : k + i + 1, :], 8)) for i in range(4)
            )
            at = lambda col, i: rep(col[:, k + i : k + i + 1, :], 8)
            p00, p01, p02, p03 = at(c0, 0), at(c1, 0), at(c2, 0), at(c3, 0)
            e0 = _recip(p00)
            l10, l20, l30 = p01 * e0, p02 * e0, p03 * e0
            e1 = _recip(at(c1, 1) - l10 * p01)
            p12, p13 = at(c2, 1) - l10 * p02, at(c3, 1) - l10 * p03
            l21, l31 = p12 * e1, p13 * e1
            e2 = _recip(at(c2, 2) - l20 * p02 - l21 * p12)
            p23 = at(c3, 2) - l20 * p03 - l21 * p13
            l32 = p23 * e2
            e3 = _recip(at(c3, 3) - l30 * p03 - l31 * p13 - l32 * p23)
            r1 = r1 - l10 * r0
            r2 = r2 - l20 * r0 - l21 * r1
            r3 = r3 - l30 * r0 - l31 * r1 - l32 * r2
            w0, w1, w2, w3 = e0 * r0, e1 * r1, e2 * r2, e3 * r3
            c1 = c1 - tall(l10) * c0
            c2 = c2 - tall(l20) * c0 - tall(l21) * c1
            c3 = c3 - tall(l30) * c0 - tall(l31) * c1 - tall(l32) * c2
            x = jnp.where((lane >= c) & (lane < c + 4), 0.0, x)
            x = x - c0 * tall(w0) - c1 * tall(w1) - c2 * tall(w2) - c3 * tall(w3)
            z2 = w2 - l32 * w3
            z1 = w1 - l21 * z2 - l31 * w3
            z0 = w0 - l10 * z1 - l20 * z2 - l30 * w3
            for i, z in enumerate((z0, z1, z2, w3)):
                x = jnp.where(sub == k + i, tall(z), x)
        signed = jnp.where(lane < lo, -start, start)
        inside = (lane_all >= lo) & (lane_all < lo + PANEL)
        for f in range(FOLDS):
            g_ref[f] = jnp.where(inside, 0.0, g_ref[f]) - _outer6(signed[f], x[f])
        g_ref[:, lo : lo + PANEL, :] = x


def _unpack(rows):
    b = _iota((LANE, W), 0)
    o = _iota((LANE, W), 1)
    spread = _hot(b == (o // 16) + jnp.where(o % 16 >= 8, 64, 0))
    value = _dot(rows, spread).astype(jnp.int32)
    shift = _iota(value.shape, 1) % 8
    return ((value >> shift) & 1).astype(F32).astype(BF)


def _core_prep_body(core_ref, ltc_ref, seen_ref, gram_ref):
    eye = jnp.where(_iota((RANK, RANK), 0) == _iota((RANK, RANK), 1), 1.0, 0.0)
    for f in range(FOLDS):
        core = core_ref[:, f * RANK : (f + 1) * RANK]
        core_t = core.T
        ltc_ref[f] = core_t
        gram_ref[f] = _dot(core_t, core) + eye
    for base in range(0, ROWS, 128):
        seen_ref[base : base + 128, :] = _unpack(core_ref[base : base + 128, FOLDS * RANK :])


def _core_prep(core):
    return pl.pallas_call(
        _core_prep_body,
        out_shape=(
            jax.ShapeDtypeStruct((FOLDS, RANK, ROWS), BF),
            jax.ShapeDtypeStruct((ROWS, W), BF),
            jax.ShapeDtypeStruct((FOLDS, RANK, RANK), F32),
        ),
        compiler_params=_params(),
        cost_estimate=_cost(10**9, 2 * 10**6),
        name="core_prep",
    )(core)


def _inverse_body(gram_ref, up_ref, down_ref, before_ref, after_ref, lth_ref, seen_ref, inv_ref):
    halos = (up_ref, down_ref, before_ref, after_ref)
    for f in range(FOLDS):
        halo = jnp.concatenate([r[:, f * RANK : (f + 1) * RANK] for r in halos], axis=0)
        halo_t = halo.T
        lth_ref[f] = halo_t
        inv_ref[f] = gram_ref[f] + _dot(halo_t, halo)
    at = 0
    for ref in halos:
        n = ref.shape[0]
        seen_ref[at : at + n, :] = _unpack(ref[:, FOLDS * RANK :])
        at += n
    _eliminate(inv_ref, 0, RANK)


def _inverse(gram, up, down, before, after):
    return pl.pallas_call(
        _inverse_body,
        out_shape=(
            jax.ShapeDtypeStruct((FOLDS, RANK, HALO), BF),
            jax.ShapeDtypeStruct((HALO, W), BF),
            jax.ShapeDtypeStruct((FOLDS, RANK, RANK), F32),
        ),
        compiler_params=_params(),
        cost_estimate=_cost(8 * 10**9, 4 * 10**6),
        name="gram_inverse",
    )(gram, up, down, before, after)


def _threshold(foldp, f):
    held = (foldp < 0.5) | ((foldp > f + 0.5) & (foldp < f + 1.5))
    return jnp.where(held, 1.0, 0.0).astype(BF)


def _fill(seen, thr, data, pred):
    thr = jnp.concatenate([thr] * (W // LANE), axis=1)
    return jnp.where(seen > thr, data, pred.astype(BF))


def _core_body(data_ref, seen_ref, l_ref, lt_ref, v_ref, out_ref):
    foldp = data_ref[:, W:].astype(F32)
    for f in range(FOLDS):
        pred = _dot_nt(l_ref[:, f * RANK : (f + 1) * RANK], v_ref[f])
        fill = _fill(seen_ref[...], _threshold(foldp, f), data_ref[:, :W], pred)
        out_ref[f] = _dot(lt_ref[f], fill)


def _core_cross(data, seen, lext, ltc, v):
    return pl.pallas_call(
        _core_body,
        out_shape=jax.ShapeDtypeStruct((FOLDS, RANK, W), F32),
        compiler_params=_params(),
        cost_estimate=_cost(3 * 10**9, 6 * 10**6),
        name="cross_core",
    )(data, seen, lext, ltc, v)


def _final_body(
    data_ref, up_ref, down_ref, before_ref, after_ref, seen_c_ref, seen_h_ref, lc_ref, lu_ref, ld_ref, lb_ref, la_ref,
    lth_ref, v_ref, cross_ref, inv_ref, got_ref, back_ref, new_ref,
):
    cat = lambda refs, cols: jnp.concatenate([r[:, cols] for r in refs], axis=0)
    halos = (up_ref, down_ref, before_ref, after_ref)
    halo = cat(halos, slice(0, W))
    foldp = cat(halos, slice(W, EXT)).astype(F32)
    lhalos = (lu_ref, ld_ref, lb_ref, la_ref)
    core_fold = data_ref[:, W:].astype(F32)
    chosen = jnp.zeros((ROWS, W), F32)
    for f in range(FOLDS):
        cols = slice(f * RANK, (f + 1) * RANK)
        pred = _dot_nt(cat(lhalos, cols), v_ref[f])
        fill = _fill(seen_h_ref[...], _threshold(foldp, f), halo, pred)
        cross = cross_ref[f] + _dot(lth_ref[f], fill)
        new = jnp.dot(inv_ref[f], cross, preferred_element_type=F32, precision=lax.Precision.HIGHEST)
        new_ref[f] = new
    lsel = []
    news = []
    for f in range(FOLDS):
        cols = slice(f * RANK, (f + 1) * RANK)
        mine = (core_fold > f + 0.5) & (core_fold < f + 1.5)
        lsel.append(jnp.where(mine, lc_ref[:, cols].astype(F32), 0.0).astype(BF))
        news.append(new_ref[f].astype(BF))
    chosen = _dot(jnp.concatenate(lsel, axis=1), jnp.concatenate(news, axis=0))
    known = jnp.concatenate([jnp.where(core_fold > 0.5, 0.0, 1.0).astype(BF)] * (W // LANE), axis=1)
    resid = (data_ref[:, :W].astype(F32) - chosen).astype(BF)
    resid = jnp.where(seen_c_ref[...] > known, resid, jnp.zeros_like(resid))
    step = 256
    for base in range(0, NSLOT, step):
        meta = got_ref[base : base + step, HALF:].astype(F32)
        m = _slot_rows((meta[:, 0:1], meta[:, 1:2], meta[:, 2:3]))
        half = ((_iota((step, 1), 0) + base) // CAP) % 2
        o = _iota((step, ROWS), 1)
        hot0 = _hot(o == jnp.where(half == 0, m, -1))
        hot1 = _hot(o == jnp.where(half == 1, m, -1))
        back = _dot(hot0, resid[:, :HALF]) + _dot(hot1, resid[:, HALF:])
        back_ref[base : base + step, :] = back.astype(BF)


def _final(data, halos, seen_c, seen_h, lext, lhalos, lth, v, cross, inv, got):
    return pl.pallas_call(
        _final_body,
        out_shape=(
            jax.ShapeDtypeStruct((NSLOT, HALF), BF),
            jax.ShapeDtypeStruct((FOLDS, RANK, W), F32),
        ),
        compiler_params=_params(),
        cost_estimate=_cost(4 * 10**9, 10**7),
        name="update_residual",
    )(data, *halos, seen_c, seen_h, lext, *lhalos, lth, v, cross, inv, got)


def _turn_body(new_ref, out_ref):
    out_ref[0] = new_ref[0].T


def _turn(new):
    return pl.pallas_call(
        _turn_body,
        grid=(FOLDS,),
        in_specs=[pl.BlockSpec((1, RANK, W), lambda f: (f, 0, 0))],
        out_specs=pl.BlockSpec((1, W, RANK), lambda f: (f, 0, 0)),
        out_shape=jax.ShapeDtypeStruct((FOLDS, W, RANK), F32),
        compiler_params=_params(),
        cost_estimate=_cost(10**6, 4 * 10**6),
        name="new_right",
    )(new)


def _return_body(ret_ref, place_ref, out_ref):
    step = 128
    for base in range(0, ROWS, step):
        place = place_ref[base : base + step, :1]
        r = _iota((step, NSLOT), 1)
        out_ref[base : base + step, :HALF] = _dot(_hot(r == place), ret_ref[...]).astype(BF)
        out_ref[base : base + step, HALF:] = _dot(_hot(r == place + CAP), ret_ref[...]).astype(BF)


def _give_back(ret, place):
    return pl.pallas_call(
        _return_body,
        out_shape=jax.ShapeDtypeStruct((ROWS, W), BF),
        compiler_params=_params(),
        cost_estimate=_cost(10**9, 4 * 10**6),
        name="give_back",
    )(ret, place)


def _swap(x):
    return lax.all_to_all(x, AXES, split_axis=0, concat_axis=0, tiled=True)


def local(acq_traces, route_owner, route_row, route_fold, sample_bits, left_factors, right_factors):
    line = lambda x: x.reshape(1, ROWS)
    send, place = _route(line(route_owner), line(route_row), line(route_fold), acq_traces)
    got = _swap(send)
    lext, *lparts = _lext(left_factors.reshape(ROWS, FOLDS * RANK), sample_bits)
    ltop, lbot, lleft, lright = lparts
    lup, ldown = _along(ltop, lbot, "mlong")
    ltc, seen_c, gram = _core_prep(lext)
    lpack = _pack(lup, ldown, lleft, lright, "margin_left")
    got, lpack, ltc, seen_c, gram = lax.optimization_barrier((got, lpack, ltc, seen_c, gram))
    data, top, bot, left, right = _place(got)
    top, bot, lpack = lax.optimization_barrier((top, bot, lpack))
    up, down = _along(top, bot, "mlong")
    lbefore, lafter = _along(*lpack, "mshort")
    pack = _pack(up, down, left, right, "margin_data")
    pack, gram = lax.optimization_barrier((pack, gram))
    halos = (up, down, *_along(*pack, "mshort"))
    lhalos = (lup, ldown, lbefore, lafter)
    cross = _core_cross(data, seen_c, lext, ltc, right_factors)
    lth, seen_h, inv = _inverse(gram, *lhalos)
    back, new = _final(data, halos, seen_c, seen_h, lext, lhalos, lth, right_factors, cross, inv, got)
    ret = _swap(back)
    new_right = _turn(new)
    return new_right, _give_back(ret, place)


def solution(mesh):
    in_specs = (
        P(AXES, None),
        P(AXES),
        P(AXES),
        P(AXES),
        P(AXES, None),
        P(AXES, None, None),
        P(None, AXES, None),
    )
    out_specs = (P(None, AXES, None), P(AXES, None))
    return jax.shard_map(local, mesh=mesh, in_specs=in_specs, out_specs=out_specs, check_vma=False)
```

profile of v0, /device:TPU:1, one launch (start us, length us, event | category | flops | bytes accessed | tf_op | source)
XLA Modules:
  0.0 110.4 jit_solution(5338373663946886524)
XLA Ops:
  0.6 4.5 %route.1 = (bf16[1024,640]{1,0:T(8,128)(2,1)}, s32[512,128]{1,0:T(8,128)}) custom-call(s32[1,512]{1,0:T(1,128)} %bitcast.18, s32[1,512]{1,0:T(1,128)} %bitcast.19, s32[1,512]{1,0:T(1,128)} %bitcast.20, bf16[512,1024]{1,0:T(8,128)(2,1)} %tr_ref.1), custom_call_target="tpu_custom_call" | custom-call | flops 1000000000 | bytes 4000000 | tf_op jit(solution)/shard_map/route/pallas_call | solution.py:97
  5.1 11.5 %all-to-all-start = ((bf16[128,8,640]{2,1,0:T(8,128)(2,1)}), bf16[128,8,640]{2,1,0:T(8,128)(2,1)S(1)}, u32[]{:S(2)}, u32[]{:S(2)}) async-start(bf16[128,8,640]{2,1,0:T(8,128)(2,1)} %bitcast.16), calls=%async_computation | async-start | bytes 2621440 | tf_op jit(solution)/shard_map/all_to_all | solution.py:468
  16.8 0.4 left_rows.1
  17.3 3.5 %collective-permute-start = (bf16[128,640]{1,0:T(8,128)(2,1)S(1)}, bf16[128,640]{1,0:T(8,128)(2,1)S(1)}, u32[]{:S(2)}, u32[]{:S(2)}) collective-permute-start(bf16[128,640]{1,0:T(8,128)(2,1)S(1)} %get-tuple-element.40), channel_id=1, source_target_pairs={{0,8},{8,16},{16,24},{24,32},{32,40},{40,48},{48,56},{56,64},{64,7... | collective-permute-start | bytes 491528 | tf_op jit(solution)/shard_map/ppermute | solution.py:182
  20.9 1.9 %collective-permute-start.1 = (bf16[128,640]{1,0:T(8,128)(2,1)S(1)}, bf16[128,640]{1,0:T(8,128)(2,1)S(1)}, u32[]{:S(2)}, u32[]{:S(2)}) collective-permute-start(bf16[128,640]{1,0:T(8,128)(2,1)S(1)} %get-tuple-element.41), channel_id=1, source_target_pairs={{8,0},{16,8},{24,16},{32,24},{40,32},{48,40},{56,48},{64,56},{72,6... | collective-permute-start | bytes 491528 | tf_op jit(solution)/shard_map/ppermute | solution.py:183
  22.8 0.7 core_prep.1
  23.5 1.0 copy-done.12
  24.5 0.8 copy-done.14
  25.3 0.7 copy-done.16
  26.1 5.8 %collective-permute-done.up_ref.lu_ref = bf16[128,640]{1,0:T(8,128)(2,1)S(1)} collective-permute-done((bf16[128,640]{1,0:T(8,128)(2,1)S(1)}, bf16[128,640]{1,0:T(8,128)(2,1)S(1)}, u32[]{:S(2)}, u32[]{:S(2)}) %collective-permute-start) | collective-permute-done | bytes 163872 | tf_op jit(solution)/shard_map/ppermute | solution.py:182
  31.9 1.6 %collective-permute-done.1.down_ref.ld_ref = bf16[128,640]{1,0:T(8,128)(2,1)S(1)} collective-permute-done((bf16[128,640]{1,0:T(8,128)(2,1)S(1)}, bf16[128,640]{1,0:T(8,128)(2,1)S(1)}, u32[]{:S(2)}, u32[]{:S(2)}) %collective-permute-start.1) | collective-permute-done | bytes 163872 | tf_op jit(solution)/shard_map/ppermute | solution.py:183
  33.7 0.6 copy-done.9
  34.3 3.0 %all-to-all-done = bf16[128,8,640]{2,1,0:T(8,128)(2,1)S(1)} async-done(((bf16[128,8,640]{2,1,0:T(8,128)(2,1)}), bf16[128,8,640]{2,1,0:T(8,128)(2,1)S(1)}, u32[]{:S(2)}, u32[]{:S(2)}) %all-to-all-start) | async-done | bytes 1310752 | tf_op jit(solution)/shard_map/all_to_all | solution.py:468
  37.4 2.0 %to_grid.1 = (bf16[512,1152]{1,0:T(8,128)(2,1)S(1)}, bf16[128,1152]{1,0:T(8,128)(2,1)S(1)}, bf16[128,1152]{1,0:T(8,128)(2,1)S(1)}, bf16[64,1152]{1,0:T(8,128)(2,1)S(1)}, bf16[64,1152]{1,0:T(8,128)(2,1)S(1)}) custom-call(bf16[1024,640]{1,0:T(8,128)(2,1)S(1)} %bitcast.12), custom_call_target="tpu_custom_call" | custom-call | flops 1000000000 | bytes 4000000 | tf_op jit(solution)/shard_map/to_grid/pallas_call | solution.py:143
  39.4 4.1 %collective-permute-start.2 = (bf16[128,1152]{1,0:T(8,128)(2,1)S(1)}, bf16[128,1152]{1,0:T(8,128)(2,1)S(1)}, u32[]{:S(2)}, u32[]{:S(2)}) collective-permute-start(bf16[128,1152]{1,0:T(8,128)(2,1)S(1)} %get-tuple-element.56), channel_id=1, source_target_pairs={{0,8},{8,16},{16,24},{24,32},{32,40},{40,48},{48,56},{56,64},{64,7... | collective-permute-start | bytes 884744 | tf_op jit(solution)/shard_map/ppermute | solution.py:182
  43.4 1.9 %collective-permute-start.3 = (bf16[128,1152]{1,0:T(8,128)(2,1)S(1)}, bf16[128,1152]{1,0:T(8,128)(2,1)S(1)}, u32[]{:S(2)}, u32[]{:S(2)}) collective-permute-start(bf16[128,1152]{1,0:T(8,128)(2,1)S(1)} %get-tuple-element.57), channel_id=1, source_target_pairs={{8,0},{16,8},{24,16},{32,24},{40,32},{48,40},{56,48},{64,56},{72,6... | collective-permute-start | bytes 884744 | tf_op jit(solution)/shard_map/ppermute | solution.py:183
  45.4 2.2 %collective-permute-start.6 = (bf16[96,640]{1,0:T(8,128)(2,1)S(1)}, bf16[96,640]{1,0:T(8,128)(2,1)S(1)}, u32[]{:S(2)}, u32[]{:S(2)}) collective-permute-start(bf16[96,640]{1,0:T(8,128)(2,1)S(1)} %copy-done.10), channel_id=1, source_target_pairs={{0,1},{1,2},{2,3},{3,4},{4,5},{5,6},{6,7},{8,9},{9,10},{10,11},{11... | collective-permute-start | bytes 368648 | tf_op jit(solution)/shard_map/ppermute | solution.py:182
  47.5 1.3 %collective-permute-start.7 = (bf16[96,640]{1,0:T(8,128)(2,1)S(1)}, bf16[96,640]{1,0:T(8,128)(2,1)S(1)}, u32[]{:S(2)}, u32[]{:S(2)}) collective-permute-start(bf16[96,640]{1,0:T(8,128)(2,1)S(1)} %get-tuple-element.68), channel_id=1, source_target_pairs={{1,0},{2,1},{3,2},{4,3},{5,4},{6,5},{7,6},{9,8},{10,9},{11,10},{12... | collective-permute-start | bytes 368648 | tf_op jit(solution)/shard_map/ppermute | solution.py:183
  48.9 2.0 %cross_core.1.cross_ref = f32[4,128,1024]{2,1,0:T(8,128)S(1)} custom-call(bf16[512,1152]{1,0:T(8,128)(2,1)S(1)} %get-tuple-element.51.data_ref, bf16[512,1024]{1,0:T(8,128)(2,1)S(1)} %copy-done.13, bf16[512,640]{1,0:T(8,128)(2,1)S(1)} %get-tuple-element.46.core_ref.l_ref.lc_ref, bf16[4,128,512]{2,1,0:T(8,128)(2,1)S(1)} %copy-done.15, ...), custom_call_target="tpu_custom_call" | custom-call | flops 3000000000 | bytes 6000000 | tf_op jit(solution)/shard_map/cross_core/pallas_call | solution.py:368
  50.9 0.9 collective-permute-done.3.down_ref
  51.8 0.3 margin_data.1
  52.1 3.3 %collective-permute-start.4 = (bf16[96,1152]{1,0:T(8,128)(2,1)S(1)}, bf16[96,1152]{1,0:T(8,128)(2,1)S(1)}, u32[]{:S(2)}, u32[]{:S(2)}) collective-permute-start(bf16[96,1152]{1,0:T(8,128)(2,1)S(1)} %get-tuple-element.63), channel_id=1, source_target_pairs={{0,1},{1,2},{2,3},{3,4},{4,5},{5,6},{6,7},{8,9},{9,10},{10,11},{11... | collective-permute-start | bytes 663560 | tf_op jit(solution)/shard_map/ppermute | solution.py:182
  55.3 1.5 %collective-permute-start.5 = (bf16[96,1152]{1,0:T(8,128)(2,1)S(1)}, bf16[96,1152]{1,0:T(8,128)(2,1)S(1)}, u32[]{:S(2)}, u32[]{:S(2)}) collective-permute-start(bf16[96,1152]{1,0:T(8,128)(2,1)S(1)} %get-tuple-element.64), channel_id=1, source_target_pairs={{1,0},{2,1},{3,2},{4,3},{5,4},{6,5},{7,6},{9,8},{10,9},{11,10},{12... | collective-permute-start | bytes 663560 | tf_op jit(solution)/shard_map/ppermute | solution.py:183
  56.9 8.9 %gram_inverse.1 = (bf16[4,128,448]{2,1,0:T(8,128)(2,1)S(1)}, bf16[448,1024]{1,0:T(8,128)(2,1)S(1)}, f32[4,128,128]{2,1,0:T(8,128)S(1)}) custom-call(f32[4,128,128]{2,1,0:T(8,128)S(1)} %copy-done.17, bf16[128,640]{1,0:T(8,128)(2,1)S(1)} %collective-permute-done.up_ref.lu_ref, bf16[128,640]{1,0:T(8,128)(2,1)S(1)} %collective-permute-done.1.down_ref.ld_ref, ...), custom_call_target="tpu_custom_call" | custom-call | flops 8000000000 | bytes 4000000 | tf_op jit(solution)/shard_map/gram_inverse/pallas_call | solution.py:336
  65.8 0.9 copy-done.2
  66.7 0.9 copy-done.4
  67.6 5.7 %update_residual.1 = (bf16[1024,512]{1,0:T(8,128)(2,1)S(1)}, f32[4,128,1024]{2,1,0:T(8,128)S(1)}) custom-call(bf16[512,1152]{1,0:T(8,128)(2,1)S(1)} %get-tuple-element.51.data_ref, bf16[128,1152]{1,0:T(8,128)(2,1)S(1)} %collective-permute-done.2.up_ref, bf16[128,1152]{1,0:T(8,128)(2,1)S(1)} %collective-permute-done.3.down_ref, ...), custom_call_target="tpu_custom_call" | custom-call | flops 4000000000 | bytes 10000000 | tf_op jit(solution)/shard_map/update_residual/pallas_call | solution.py:419
  73.4 1.0 copy-done
  74.3 15.8 %all-to-all-start.1 = ((bf16[128,8,512]{2,1,0:T(8,128)(2,1)}), bf16[128,8,512]{2,1,0:T(8,128)(2,1)S(1)}, u32[]{:S(2)}, u32[]{:S(2)}) async-start(bf16[128,8,512]{2,1,0:T(8,128)(2,1)} %bitcast.14), calls=%async_computation.1 | async-start | bytes 2097152 | tf_op jit(solution)/shard_map/all_to_all | solution.py:468
  90.1 2.2 %new_right.1 = f32[4,1024,128]{2,1,0:T(8,128)} custom-call(f32[4,128,1024]{2,1,0:T(8,128)S(1)} %get-tuple-element.73.new_ref), custom_call_target="tpu_custom_call" | custom-call | flops 1000000 | bytes 4000000 | tf_op jit(solution)/shard_map/new_right/pallas_call | solution.py:436
  92.3 15.8 %all-to-all-done.1 = bf16[128,8,512]{2,1,0:T(8,128)(2,1)S(1)} async-done(((bf16[128,8,512]{2,1,0:T(8,128)(2,1)}), bf16[128,8,512]{2,1,0:T(8,128)(2,1)S(1)}, u32[]{:S(2)}, u32[]{:S(2)}) %all-to-all-start.1) | async-done | bytes 1048608 | tf_op jit(solution)/shard_map/all_to_all | solution.py:468
  108.1 2.3 %give_back.1 = bf16[512,1024]{1,0:T(8,128)(2,1)} custom-call(bf16[1024,512]{1,0:T(8,128)(2,1)S(1)} %bitcast.15, s32[512,128]{1,0:T(8,128)S(1)} %copy-done.11), custom_call_target="tpu_custom_call" | custom-call | flops 1000000000 | bytes 4000000 | tf_op jit(solution)/shard_map/give_back/pallas_call | solution.py:458
  (41 shorter events, 0.5 us)
Async XLA Ops:
  5.1 11.5 %copy-start.19 = (s32[512,64]{0,1:T(8,128)S(1)}, s32[512,64]{0,1:T(8,128)}, u32[]{:S(2)}) copy-start(s32[512,64]{0,1:T(8,128)} %param.11) | copy-start | bytes 393220
  5.1 11.7 %copy-start.18 = (bf16[512,4,128]{2,1,0:T(4,128)(2,1)S(1)}, bf16[512,4,128]{2,1,0:T(4,128)(2,1)}, u32[]{:S(2)}) copy-start(bf16[512,4,128]{2,1,0:T(4,128)(2,1)} %param.12) | copy-start | bytes 1572868
  5.1 32.3 %all-to-all-start = ((bf16[128,8,640]{2,1,0:T(8,128)(2,1)}), bf16[128,8,640]{2,1,0:T(8,128)(2,1)S(1)}, u32[]{:S(2)}, u32[]{:S(2)}) async-start(bf16[128,8,640]{2,1,0:T(8,128)(2,1)} %bitcast.16), calls=%async_computation | async-start | bytes 2621440 | tf_op jit(solution)/shard_map/all_to_all | solution.py:468
  17.3 31.6 %copy-start.7 = (bf16[512,640]{1,0:T(8,128)(2,1)}, bf16[512,640]{1,0:T(8,128)(2,1)S(1)}, u32[]{:S(2)}) copy-start(bf16[512,640]{1,0:T(8,128)(2,1)S(1)} %get-tuple-element.46.core_ref.l_ref.lc_ref) | copy-start | bytes 1966084
  17.3 14.6 %collective-permute-start = (bf16[128,640]{1,0:T(8,128)(2,1)S(1)}, bf16[128,640]{1,0:T(8,128)(2,1)S(1)}, u32[]{:S(2)}, u32[]{:S(2)}) collective-permute-start(bf16[128,640]{1,0:T(8,128)(2,1)S(1)} %get-tuple-element.40), channel_id=1, source_target_pairs={{0,8},{8,16},{16,24},{24,32},{32,40},{40,48},{48,56},{56,64},{64,7... | collective-permute-start | bytes 491528 | tf_op jit(solution)/shard_map/ppermute | solution.py:182
  20.9 12.6 %collective-permute-start.1 = (bf16[128,640]{1,0:T(8,128)(2,1)S(1)}, bf16[128,640]{1,0:T(8,128)(2,1)S(1)}, u32[]{:S(2)}, u32[]{:S(2)}) collective-permute-start(bf16[128,640]{1,0:T(8,128)(2,1)S(1)} %get-tuple-element.41), channel_id=1, source_target_pairs={{8,0},{16,8},{24,16},{32,24},{40,32},{48,40},{56,48},{64,56},{72,6... | collective-permute-start | bytes 491528 | tf_op jit(solution)/shard_map/ppermute | solution.py:183
  23.5 1.0 copy-start.12
  24.5 0.8 copy-start.14
  25.3 0.7 copy-start.16
  31.9 25.0 %copy-start.1 = (bf16[128,640]{1,0:T(8,128)(2,1)}, bf16[128,640]{1,0:T(8,128)(2,1)S(1)}, u32[]{:S(2)}) copy-start(bf16[128,640]{1,0:T(8,128)(2,1)S(1)} %collective-permute-done.up_ref.lu_ref) | copy-start | bytes 491524
  33.5 23.4 %copy-start.3 = (bf16[128,640]{1,0:T(8,128)(2,1)}, bf16[128,640]{1,0:T(8,128)(2,1)S(1)}, u32[]{:S(2)}) copy-start(bf16[128,640]{1,0:T(8,128)(2,1)S(1)} %collective-permute-done.1.down_ref.ld_ref) | copy-start | bytes 491524
  33.5 15.4 %copy-start.5 = (bf16[4,1024,128]{2,1,0:T(8,128)(2,1)S(1)}, bf16[4,1024,128]{2,1,0:T(8,128)(2,1)}, u32[]{:S(2)}) copy-start(bf16[4,1024,128]{2,1,0:T(8,128)(2,1)} %v_ref.3) | copy-start | bytes 3145732
  33.7 0.7 copy-start.9
  37.4 8.0 %copy-start.10 = (bf16[96,640]{1,0:T(8,128)(2,1)S(1)}, bf16[96,640]{1,0:T(8,128)(2,1)}, u32[]{:S(2)}) copy-start(bf16[96,640]{1,0:T(8,128)(2,1)} %copy-done.9) | copy-start | bytes 368644
  37.4 11.5 %copy-start.13 = (bf16[512,1024]{1,0:T(8,128)(2,1)S(1)}, bf16[512,1024]{1,0:T(8,128)(2,1)}, u32[]{:S(2)}) copy-start(bf16[512,1024]{1,0:T(8,128)(2,1)} %copy-done.12) | copy-start | bytes 3145732
  37.4 11.5 %copy-start.15 = (bf16[4,128,512]{2,1,0:T(8,128)(2,1)S(1)}, bf16[4,128,512]{2,1,0:T(8,128)(2,1)}, u32[]{:S(2)}) copy-start(bf16[4,128,512]{2,1,0:T(8,128)(2,1)} %copy-done.14) | copy-start | bytes 1572868
  39.4 11.5 %collective-permute-start.2 = (bf16[128,1152]{1,0:T(8,128)(2,1)S(1)}, bf16[128,1152]{1,0:T(8,128)(2,1)S(1)}, u32[]{:S(2)}, u32[]{:S(2)}) collective-permute-start(bf16[128,1152]{1,0:T(8,128)(2,1)S(1)} %get-tuple-element.56), channel_id=1, source_target_pairs={{0,8},{8,16},{16,24},{24,32},{32,40},{40,48},{48,56},{56,64},{64,7... | collective-permute-start | bytes 884744 | tf_op jit(solution)/shard_map/ppermute | solution.py:182
  43.4 8.3 %collective-permute-start.3 = (bf16[128,1152]{1,0:T(8,128)(2,1)S(1)}, bf16[128,1152]{1,0:T(8,128)(2,1)S(1)}, u32[]{:S(2)}, u32[]{:S(2)}) collective-permute-start(bf16[128,1152]{1,0:T(8,128)(2,1)S(1)} %get-tuple-element.57), channel_id=1, source_target_pairs={{8,0},{16,8},{24,16},{32,24},{40,32},{48,40},{56,48},{64,56},{72,6... | collective-permute-start | bytes 884744 | tf_op jit(solution)/shard_map/ppermute | solution.py:183
  45.4 11.5 %collective-permute-start.6 = (bf16[96,640]{1,0:T(8,128)(2,1)S(1)}, bf16[96,640]{1,0:T(8,128)(2,1)S(1)}, u32[]{:S(2)}, u32[]{:S(2)}) collective-permute-start(bf16[96,640]{1,0:T(8,128)(2,1)S(1)} %copy-done.10), channel_id=1, source_target_pairs={{0,1},{1,2},{2,3},{3,4},{4,5},{5,6},{6,7},{8,9},{9,10},{10,11},{11... | collective-permute-start | bytes 368648 | tf_op jit(solution)/shard_map/ppermute | solution.py:182
  47.5 9.3 %collective-permute-start.7 = (bf16[96,640]{1,0:T(8,128)(2,1)S(1)}, bf16[96,640]{1,0:T(8,128)(2,1)S(1)}, u32[]{:S(2)}, u32[]{:S(2)}) collective-permute-start(bf16[96,640]{1,0:T(8,128)(2,1)S(1)} %get-tuple-element.68), channel_id=1, source_target_pairs={{1,0},{2,1},{3,2},{4,3},{5,4},{6,5},{7,6},{9,8},{10,9},{11,10},{12... | collective-permute-start | bytes 368648 | tf_op jit(solution)/shard_map/ppermute | solution.py:183
  48.9 8.0 %copy-start.17 = (f32[4,128,128]{2,1,0:T(8,128)S(1)}, f32[4,128,128]{2,1,0:T(8,128)}, u32[]{:S(2)}) copy-start(f32[4,128,128]{2,1,0:T(8,128)} %copy-done.16) | copy-start | bytes 786436
  52.0 13.7 %copy-start.6 = (bf16[4,1024,128]{2,1,0:T(8,128)(2,1)S(1)}, bf16[4,1024,128]{2,1,0:T(8,128)(2,1)}, u32[]{:S(2)}) copy-start(bf16[4,1024,128]{2,1,0:T(8,128)(2,1)} %v_ref.3) | copy-start | bytes 3145732
  52.0 13.8 %copy-start.8 = (bf16[512,640]{1,0:T(8,128)(2,1)S(1)}, bf16[512,640]{1,0:T(8,128)(2,1)}, u32[]{:S(2)}) copy-start(bf16[512,640]{1,0:T(8,128)(2,1)} %copy-done.7) | copy-start | bytes 1966084
  52.1 13.7 %collective-permute-start.4 = (bf16[96,1152]{1,0:T(8,128)(2,1)S(1)}, bf16[96,1152]{1,0:T(8,128)(2,1)S(1)}, u32[]{:S(2)}, u32[]{:S(2)}) collective-permute-start(bf16[96,1152]{1,0:T(8,128)(2,1)S(1)} %get-tuple-element.63), channel_id=1, source_target_pairs={{0,1},{1,2},{2,3},{3,4},{4,5},{5,6},{6,7},{8,9},{9,10},{10,11},{11... | collective-permute-start | bytes 663560 | tf_op jit(solution)/shard_map/ppermute | solution.py:182
  55.3 10.4 %collective-permute-start.5 = (bf16[96,1152]{1,0:T(8,128)(2,1)S(1)}, bf16[96,1152]{1,0:T(8,128)(2,1)S(1)}, u32[]{:S(2)}, u32[]{:S(2)}) collective-permute-start(bf16[96,1152]{1,0:T(8,128)(2,1)S(1)} %get-tuple-element.64), channel_id=1, source_target_pairs={{1,0},{2,1},{3,2},{4,3},{5,4},{6,5},{7,6},{9,8},{10,9},{11,10},{12... | collective-permute-start | bytes 663560 | tf_op jit(solution)/shard_map/ppermute | solution.py:183
  65.8 0.9 copy-start.2
  66.7 0.9 copy-start.4
  73.4 1.0 copy-start
  74.3 33.8 %all-to-all-start.1 = ((bf16[128,8,512]{2,1,0:T(8,128)(2,1)}), bf16[128,8,512]{2,1,0:T(8,128)(2,1)S(1)}, u32[]{:S(2)}, u32[]{:S(2)}) async-start(bf16[128,8,512]{2,1,0:T(8,128)(2,1)} %bitcast.14), calls=%async_computation.1 | async-start | bytes 2097152 | tf_op jit(solution)/shard_map/all_to_all | solution.py:468
  90.1 18.0 %copy-start.11 = (s32[512,128]{1,0:T(8,128)S(1)}, s32[512,128]{1,0:T(8,128)}, u32[]{:S(2)}) copy-start(s32[512,128]{1,0:T(8,128)} %get-tuple-element.75.place_ref) | copy-start | bytes 786436
where the time goes:
time: 111 us; the launch traced here: 110 us
  starting transfers between devices  46.9 us (42%)
  Pallas kernels  29.2 us (26%)
  waiting for transfers between devices  27.1 us (24%)
  local copies, waits for them, and re-layouts  6.21 us (6%)
    all_to_all x2, starting transfers between devices, _swap(): return lax.all_to_all(x, AXES, split_axis=0, concat_axis=0, tiled=True)  27.3 us
    all_to_all x2, waiting for transfers between devices, _swap(): return lax.all_to_all(x, AXES, split_axis=0, concat_axis=0, tiled=True)  18.8 us
    ppermute x4, starting transfers between devices, _along(): before = lax.ppermute(to_down, axis, fwd)  13 us
    pallas_call x1, Pallas kernels, _inverse(): pl.pallas_call(_inverse_body, out_shape=(jax.ShapeDtypeStruct((FOLDS, RAN...  8.89 us
    ppermute x4, starting transfers between devices, _along(): after = lax.ppermute(to_up, axis, [(j, i) for i, j in fwd])  6.61 us
    unnamed x42, local copies, waits for them, and re-layouts  6.21 us
    ppermute x4, waiting for transfers between devices, _along(): before = lax.ppermute(to_down, axis, fwd)  5.84 us
    pallas_call x1, Pallas kernels, _final(): pl.pallas_call(_final_body, out_shape=(jax.ShapeDtypeStruct((NSLOT, HALF)...  5.72 us
  transfers between devices with their start and end apart: 10, of which 5 were waited for; matrix products, arithmetic and copies ran while one was open for 0% of the time, Pallas kernels for 13%

commit v1 on v0

--- a/solution.py
+++ b/solution.py
@@ -1,3 +1,5 @@
+import functools
+
 import jax
 import jax.numpy as jnp
 from jax import lax
@@ -21,9 +23,10 @@
 LEXT = FOLDS * RANK + LANE
 STRIP = H * CY
 SIDE = H * CX
-TALL = H * (CX + 2 * H)
-HALO = 2 * STRIP + 2 * TALL
+WIDE = H * (CY + 2 * H)
+HALO = 2 * SIDE + 2 * WIDE
 PANEL = 16
+SPLIT = 64
 
 BF = jnp.bfloat16
 F32 = jnp.float32
@@ -52,6 +55,19 @@
 
 def _cost(flops, nbytes):
     return pl.CostEstimate(flops=flops, bytes_accessed=nbytes, transcendentals=0)
+
+
+_VMEM = pl.BlockSpec(memory_space=pltpu.VMEM)
+_HBM = pl.BlockSpec(memory_space=pltpu.HBM)
+_ANY = pl.BlockSpec(memory_space=pl.ANY)
+
+
+def _weave(y):
+    y = y.reshape(y.shape[0] // SLOT, SLOT, W)
+    left, right = y[:, :, :HALF], y[:, :, HALF:]
+    even = jnp.concatenate([left[:, :CAP], right[:, :CAP]], axis=1)
+    odd = jnp.concatenate([left[:, CAP:], right[:, CAP:]], axis=1)
+    return jnp.stack([even, odd], axis=1).reshape(-1, HALF)
 
 
 def _side_select(shape, first):
@@ -60,7 +76,19 @@
     return _hot(m == (r // H) * CY + first + r % H)
 
 
-def _route_body(own_ref, row_ref, fold_ref, tr_ref, send_ref, place_ref):
+def _route_body(
+    own_hbm, row_hbm, fold_hbm, tr_hbm, send_hbm, place_ref, own_ref, row_ref, fold_ref, tr_ref, send_ref, in_sem, out_sem
+):
+    notes = [
+        pltpu.make_async_copy(src, dst, in_sem.at[i])
+        for i, (src, dst) in enumerate(((own_hbm, own_ref), (row_hbm, row_ref), (fold_hbm, fold_ref)))
+    ]
+    for note in notes:
+        note.start()
+    load = pltpu.make_async_copy(tr_hbm, tr_ref, in_sem.at[3])
+    load.start()
+    for note in notes:
+        note.wait()
     own = own_ref[...]
     row = row_ref[...]
     valid = own >= 0
@@ -78,28 +106,47 @@
     rs = _iota((ROWS, ROWS), 0)
     cs = _iota((ROWS, ROWS), 1)
     within = jnp.sum(jnp.where(same & (rs < cs), 1.0, 0.0), axis=0, keepdims=True)
-    place = jnp.where(valid, ownf * SLOT + within, -64.0).astype(jnp.int32)
+    place = jnp.where(valid, ownf * CAP + within, -64.0).astype(jnp.int32)
     within_c = jnp.sum(jnp.where(same & (cs < rs), 1.0, 0.0), axis=1, keepdims=True)
     place_c = jnp.where(ocol >= 0.0, ocol * SLOT + within_c, -64.0)
     place_ref[...] = jnp.broadcast_to(place_c, (ROWS, LANE)).astype(jnp.int32)
     meta_b = meta_t.astype(BF)
-    step = 256
-    for base in range(0, NSLOT, step):
-        r = _iota((step, ROWS), 0) + base
-        hot0 = _hot(r == place)
-        hot1 = _hot(r == place + CAP)
-        y = _dot(hot0, tr_ref[:, :HALF]) + _dot(hot1, tr_ref[:, HALF:])
-        send_ref[base : base + step, :HALF] = y.astype(BF)
-        send_ref[base : base + step, HALF:] = _dot(hot0 + hot1, meta_b).astype(BF)
+    load.wait()
+    step = 128
+    stores = []
+    for i, base in enumerate(range(0, ROWS, step)):
+        hot = _hot(_iota((step, ROWS), 0) + base == place)
+        note = _dot(hot, meta_b)
+        y = _weave(_dot(hot, tr_ref[...]))
+        note = _weave(jnp.concatenate([note] * (W // LANE), axis=1))[:, :LANE]
+        out = slice(2 * base, 2 * (base + step))
+        send_ref[out, :HALF] = y.astype(BF)
+        send_ref[out, HALF:] = note.astype(BF)
+        store = pltpu.make_async_copy(send_ref.at[out], send_hbm.at[out], out_sem.at[i])
+        store.start()
+        stores.append(store)
+    for store in stores:
+        store.wait()
 
 
 def _route(own, row, fold, traces):
     return pl.pallas_call(
         _route_body,
-        out_shape=(
-            jax.ShapeDtypeStruct((NSLOT, HALF + LANE), BF),
+        in_specs=[_HBM] * 4,
+        out_specs=(_HBM, _VMEM),
+        out_shape=(
+            pltpu.HBM((NSLOT, HALF + LANE), BF),
             jax.ShapeDtypeStruct((ROWS, LANE), jnp.int32),
         ),
+        scratch_shapes=[
+            pltpu.VMEM((1, ROWS), jnp.int32),
+            pltpu.VMEM((1, ROWS), jnp.int32),
+            pltpu.VMEM((1, ROWS), jnp.int32),
+            pltpu.VMEM((ROWS, W), BF),
+            pltpu.VMEM((NSLOT, HALF + LANE), BF),
+            pltpu.SemaphoreType.DMA((4,)),
+            pltpu.SemaphoreType.DMA((4,)),
+        ],
         compiler_params=_params(60),
         cost_estimate=_cost(10**9, 4 * 10**6),
         name="route",
@@ -110,7 +157,7 @@
     return jnp.where(meta[0] > 0.5, meta[1] * CY + meta[2], -1.0).astype(jnp.int32)
 
 
-def _place_body(got_ref, core_ref, top_ref, bot_ref, left_ref, right_ref):
+def _place_body(got_ref, after_ref, core_ref, top_ref, bot_ref, left_ref, right_ref):
     meta = got_ref[:, HALF:].astype(F32).T
     m = _slot_rows((meta[0:1], meta[1:2], meta[2:3]))
     half = (_iota((1, NSLOT), 1) // CAP) % 2
@@ -139,9 +186,10 @@
     right_ref[...] = _dot(_side_select((SIDE, ROWS), CY - H), core).astype(BF)
 
 
-def _place(got):
+def _place(got, after):
     return pl.pallas_call(
         _place_body,
+        in_specs=[_VMEM, _ANY],
         out_shape=(
             jax.ShapeDtypeStruct((ROWS, EXT), BF),
             jax.ShapeDtypeStruct((STRIP, EXT), BF),
@@ -152,36 +200,45 @@
         compiler_params=_params(),
         cost_estimate=_cost(10**9, 4 * 10**6),
         name="to_grid",
-    )(got)
-
-
-def _pack_body(up_ref, down_ref, left_ref, right_ref, to_left_ref, to_right_ref):
-    for first, side, out in ((0, left_ref, to_left_ref), (CY - H, right_ref, to_right_ref)):
-        pick = _side_select((H * H, STRIP), first)
-        out[: H * H, :] = _dot(pick, up_ref[...]).astype(BF)
-        out[H * H : H * H + SIDE, :] = side[...]
-        out[H * H + SIDE :, :] = _dot(pick, down_ref[...]).astype(BF)
-
-
-def _pack(up, down, left, right, name):
-    width = up.shape[1]
-    return pl.pallas_call(
-        _pack_body,
-        out_shape=(
-            jax.ShapeDtypeStruct((TALL, width), BF),
-            jax.ShapeDtypeStruct((TALL, width), BF),
+    )(got, after)
+
+
+def _pack_body(cut, before_ref, after_ref, top_ref, bot_ref, token_ref, to_up_ref, to_down_ref):
+    keep = _inner("mlong") if cut else (None, None)
+    far = SIDE - H * H
+    for at, strip, out, inner in ((0, top_ref, to_up_ref, keep[0]), (far, bot_ref, to_down_ref, keep[1])):
+        edge = (lambda x: (x.astype(F32) * inner).astype(BF)) if cut else (lambda x: x)
+        out[: H * H, :] = edge(before_ref[at : at + H * H, :])
+        out[H * H : H * H + STRIP, :] = edge(strip[...])
+        out[H * H + STRIP :, :] = edge(after_ref[at : at + H * H, :])
+
+
+def _pack(before, after, top, bot, token, cut, name):
+    width = top.shape[1]
+    return pl.pallas_call(
+        functools.partial(_pack_body, cut),
+        in_specs=[_VMEM] * 4 + [_ANY],
+        out_shape=(
+            jax.ShapeDtypeStruct((WIDE, width), BF),
+            jax.ShapeDtypeStruct((WIDE, width), BF),
         ),
         compiler_params=_params(),
         cost_estimate=_cost(10**7, 10**6),
         name=name,
-    )(up, down, left, right)
+    )(before, after, top, bot, token)
 
 
 def _along(to_up, to_down, axis):
-    fwd = [(i, i + 1) for i in range(lax.axis_size(axis) - 1)]
+    n = lax.axis_size(axis)
+    fwd = [(i, (i + 1) % n) for i in range(n)]
     before = lax.ppermute(to_down, axis, fwd)
     after = lax.ppermute(to_up, axis, [(j, i) for i, j in fwd])
     return before, after
+
+
+def _inner(axis):
+    at = lax.axis_index(axis)
+    return jnp.where(at > 0, 1.0, 0.0), jnp.where(at < lax.axis_size(axis) - 1, 1.0, 0.0)
 
 
 def _lext_body(left_ref, bits_ref, core_ref, top_ref, bot_ref, lside_ref, rside_ref):
@@ -191,10 +248,11 @@
     high = (bits >> 8).astype(F32)
     core_ref[:, FOLDS * RANK :] = jnp.concatenate([low, high], axis=1).astype(BF)
     core = core_ref[...]
+    before, after = _inner("mshort")
     top_ref[...] = core[:STRIP]
     bot_ref[...] = core[ROWS - STRIP :]
-    lside_ref[...] = _dot(_side_select((SIDE, ROWS), 0), core).astype(BF)
-    rside_ref[...] = _dot(_side_select((SIDE, ROWS), CY - H), core).astype(BF)
+    lside_ref[...] = (_dot(_side_select((SIDE, ROWS), 0), core) * before).astype(BF)
+    rside_ref[...] = (_dot(_side_select((SIDE, ROWS), CY - H), core) * after).astype(BF)
 
 
 def _lext(left, bits):
@@ -215,7 +273,6 @@
 
 def _recip(x):
     r = pl.reciprocal(x, approx=True)
-    r = r * (2.0 - x * r)
     return r * (2.0 - x * r)
 
 
@@ -292,7 +349,8 @@
     return ((value >> shift) & 1).astype(F32).astype(BF)
 
 
-def _core_prep_body(core_ref, ltc_ref, seen_ref, gram_ref):
+def _core_prep_body(core_ref, ltc_ref, seen_ref, gram_ref, token_ref):
+    token_ref[...] = jnp.zeros_like(token_ref)
     eye = jnp.where(_iota((RANK, RANK), 0) == _iota((RANK, RANK), 1), 1.0, 0.0)
     for f in range(FOLDS):
         core = core_ref[:, f * RANK : (f + 1) * RANK]
@@ -310,6 +368,7 @@
             jax.ShapeDtypeStruct((FOLDS, RANK, ROWS), BF),
             jax.ShapeDtypeStruct((ROWS, W), BF),
             jax.ShapeDtypeStruct((FOLDS, RANK, RANK), F32),
+            jax.ShapeDtypeStruct((8, LANE), F32),
         ),
         compiler_params=_params(),
         cost_estimate=_cost(10**9, 2 * 10**6),
@@ -317,33 +376,52 @@
     )(core)
 
 
-def _inverse_body(gram_ref, up_ref, down_ref, before_ref, after_ref, lth_ref, seen_ref, inv_ref):
-    halos = (up_ref, down_ref, before_ref, after_ref)
+def _inverse_first_body(gram_ref, before_ref, after_ref, up_ref, down_ref, v_ref, token_ref, lth_ref, seen_ref, pred_ref, part_ref):
+    halos = (before_ref, after_ref, up_ref, down_ref)
     for f in range(FOLDS):
         halo = jnp.concatenate([r[:, f * RANK : (f + 1) * RANK] for r in halos], axis=0)
         halo_t = halo.T
         lth_ref[f] = halo_t
-        inv_ref[f] = gram_ref[f] + _dot(halo_t, halo)
+        part_ref[f] = gram_ref[f] + _dot(halo_t, halo)
+        pred_ref[f] = _dot_nt(halo, v_ref[f]).astype(BF)
     at = 0
     for ref in halos:
         n = ref.shape[0]
         seen_ref[at : at + n, :] = _unpack(ref[:, FOLDS * RANK :])
         at += n
-    _eliminate(inv_ref, 0, RANK)
-
-
-def _inverse(gram, up, down, before, after):
-    return pl.pallas_call(
-        _inverse_body,
+    _eliminate(part_ref, 0, SPLIT)
+
+
+def _inverse_first(gram, before, after, up, down, v, token):
+    return pl.pallas_call(
+        _inverse_first_body,
+        in_specs=[_VMEM] * 6 + [_ANY],
         out_shape=(
             jax.ShapeDtypeStruct((FOLDS, RANK, HALO), BF),
             jax.ShapeDtypeStruct((HALO, W), BF),
+            jax.ShapeDtypeStruct((FOLDS, HALO, W), BF),
             jax.ShapeDtypeStruct((FOLDS, RANK, RANK), F32),
         ),
         compiler_params=_params(),
-        cost_estimate=_cost(8 * 10**9, 4 * 10**6),
-        name="gram_inverse",
-    )(gram, up, down, before, after)
+        cost_estimate=_cost(4 * 10**9, 4 * 10**6),
+        name="inverse_first",
+    )(gram, before, after, up, down, v, token)
+
+
+def _inverse_second_body(part_ref, token_ref, inv_ref):
+    inv_ref[...] = part_ref[...]
+    _eliminate(inv_ref, SPLIT, RANK)
+
+
+def _inverse_second(part, token):
+    return pl.pallas_call(
+        _inverse_second_body,
+        in_specs=[_VMEM, _ANY],
+        out_shape=jax.ShapeDtypeStruct((FOLDS, RANK, RANK), F32),
+        compiler_params=_params(),
+        cost_estimate=_cost(4 * 10**9, 10**6),
+        name="inverse_second",
+    )(part, token)
 
 
 def _threshold(foldp, f):
@@ -375,23 +453,18 @@
 
 
 def _final_body(
-    data_ref, up_ref, down_ref, before_ref, after_ref, seen_c_ref, seen_h_ref, lc_ref, lu_ref, ld_ref, lb_ref, la_ref,
-    lth_ref, v_ref, cross_ref, inv_ref, got_ref, back_ref, new_ref,
+    data_ref, before_ref, after_ref, up_ref, down_ref, seen_c_ref, seen_h_ref, lc_ref, lth_ref, pred_ref, cross_ref, inv_ref,
+    got_ref, back_hbm, new_ref, back_ref, sem,
 ):
     cat = lambda refs, cols: jnp.concatenate([r[:, cols] for r in refs], axis=0)
-    halos = (up_ref, down_ref, before_ref, after_ref)
+    halos = (before_ref, after_ref, up_ref, down_ref)
     halo = cat(halos, slice(0, W))
     foldp = cat(halos, slice(W, EXT)).astype(F32)
-    lhalos = (lu_ref, ld_ref, lb_ref, la_ref)
     core_fold = data_ref[:, W:].astype(F32)
-    chosen = jnp.zeros((ROWS, W), F32)
     for f in range(FOLDS):
-        cols = slice(f * RANK, (f + 1) * RANK)
-        pred = _dot_nt(cat(lhalos, cols), v_ref[f])
-        fill = _fill(seen_h_ref[...], _threshold(foldp, f), halo, pred)
+        fill = _fill(seen_h_ref[...], _threshold(foldp, f), halo, pred_ref[f])
         cross = cross_ref[f] + _dot(lth_ref[f], fill)
-        new = jnp.dot(inv_ref[f], cross, preferred_element_type=F32, precision=lax.Precision.HIGHEST)
-        new_ref[f] = new
+        new_ref[f] = jnp.dot(inv_ref[f], cross, preferred_element_type=F32, precision=lax.Precision.HIGHEST)
     lsel = []
     news = []
     for f in range(FOLDS):
@@ -403,29 +476,35 @@
     known = jnp.concatenate([jnp.where(core_fold > 0.5, 0.0, 1.0).astype(BF)] * (W // LANE), axis=1)
     resid = (data_ref[:, :W].astype(F32) - chosen).astype(BF)
     resid = jnp.where(seen_c_ref[...] > known, resid, jnp.zeros_like(resid))
-    step = 256
-    for base in range(0, NSLOT, step):
-        meta = got_ref[base : base + step, HALF:].astype(F32)
-        m = _slot_rows((meta[:, 0:1], meta[:, 1:2], meta[:, 2:3]))
-        half = ((_iota((step, 1), 0) + base) // CAP) % 2
-        o = _iota((step, ROWS), 1)
-        hot0 = _hot(o == jnp.where(half == 0, m, -1))
-        hot1 = _hot(o == jnp.where(half == 1, m, -1))
-        back = _dot(hot0, resid[:, :HALF]) + _dot(hot1, resid[:, HALF:])
-        back_ref[base : base + step, :] = back.astype(BF)
-
-
-def _final(data, halos, seen_c, seen_h, lext, lhalos, lth, v, cross, inv, got):
+    meta = got_ref[:, HALF:].astype(F32).reshape(LANE, 2, CAP, LANE)[:, 0].reshape(ROWS, LANE)
+    m = _slot_rows((meta[:, 0:1], meta[:, 1:2], meta[:, 2:3]))
+    step = 128
+    stores = []
+    for i, base in enumerate(range(0, ROWS, step)):
+        hot = _hot(_iota((step, ROWS), 1) == m[base : base + step])
+        out = slice(2 * base, 2 * (base + step))
+        back_ref[out, :] = _weave(_dot(hot, resid)).astype(BF)
+        store = pltpu.make_async_copy(back_ref.at[out], back_hbm.at[out], sem.at[i])
+        store.start()
+        stores.append(store)
+    for store in stores:
+        store.wait()
+
+
+def _final(data, halos, seen_c, seen_h, lext, lth, pred, cross, inv, got):
     return pl.pallas_call(
         _final_body,
-        out_shape=(
-            jax.ShapeDtypeStruct((NSLOT, HALF), BF),
+        in_specs=[_VMEM] * 13,
+        out_specs=(_HBM, _VMEM),
+        scratch_shapes=[pltpu.VMEM((NSLOT, HALF), BF), pltpu.SemaphoreType.DMA((4,))],
+        out_shape=(
+            pltpu.HBM((NSLOT, HALF), BF),
             jax.ShapeDtypeStruct((FOLDS, RANK, W), F32),
         ),
         compiler_params=_params(),
         cost_estimate=_cost(4 * 10**9, 10**7),
         name="update_residual",
-    )(data, *halos, seen_c, seen_h, lext, *lhalos, lth, v, cross, inv, got)
+    )(data, *halos, seen_c, seen_h, lext, lth, pred, cross, inv, got)
 
 
 def _turn_body(new_ref, out_ref):
@@ -445,19 +524,29 @@
     )(new)
 
 
-def _return_body(ret_ref, place_ref, out_ref):
+def _return_body(ret_ref, place_ref, out_hbm, out_ref, sem):
     step = 128
-    for base in range(0, ROWS, step):
-        place = place_ref[base : base + step, :1]
+    stores = []
+    for i, base in enumerate(range(0, ROWS, step)):
+        out = slice(base, base + step)
+        place = place_ref[out, :1]
         r = _iota((step, NSLOT), 1)
-        out_ref[base : base + step, :HALF] = _dot(_hot(r == place), ret_ref[...]).astype(BF)
-        out_ref[base : base + step, HALF:] = _dot(_hot(r == place + CAP), ret_ref[...]).astype(BF)
+        out_ref[out, :HALF] = _dot(_hot(r == place), ret_ref[...]).astype(BF)
+        out_ref[out, HALF:] = _dot(_hot(r == place + CAP), ret_ref[...]).astype(BF)
+        store = pltpu.make_async_copy(out_ref.at[out], out_hbm.at[out], sem.at[i])
+        store.start()
+        stores.append(store)
+    for store in stores:
+        store.wait()
 
 
 def _give_back(ret, place):
     return pl.pallas_call(
         _return_body,
-        out_shape=jax.ShapeDtypeStruct((ROWS, W), BF),
+        in_specs=[_VMEM, _VMEM],
+        out_specs=_HBM,
+        out_shape=pltpu.HBM((ROWS, W), BF),
+        scratch_shapes=[pltpu.VMEM((ROWS, W), BF), pltpu.SemaphoreType.DMA((4,))],
         compiler_params=_params(),
         cost_estimate=_cost(10**9, 4 * 10**6),
         name="give_back",
@@ -472,23 +561,19 @@
     line = lambda x: x.reshape(1, ROWS)
     send, place = _route(line(route_owner), line(route_row), line(route_fold), acq_traces)
     got = _swap(send)
-    lext, *lparts = _lext(left_factors.reshape(ROWS, FOLDS * RANK), sample_bits)
-    ltop, lbot, lleft, lright = lparts
-    lup, ldown = _along(ltop, lbot, "mlong")
-    ltc, seen_c, gram = _core_prep(lext)
-    lpack = _pack(lup, ldown, lleft, lright, "margin_left")
-    got, lpack, ltc, seen_c, gram = lax.optimization_barrier((got, lpack, ltc, seen_c, gram))
-    data, top, bot, left, right = _place(got)
-    top, bot, lpack = lax.optimization_barrier((top, bot, lpack))
-    up, down = _along(top, bot, "mlong")
-    lbefore, lafter = _along(*lpack, "mshort")
-    pack = _pack(up, down, left, right, "margin_data")
-    pack, gram = lax.optimization_barrier((pack, gram))
-    halos = (up, down, *_along(*pack, "mshort"))
-    lhalos = (lup, ldown, lbefore, lafter)
+    lext, ltop, lbot, lleft, lright = _lext(left_factors.reshape(ROWS, FOLDS * RANK), sample_bits)
+    lbefore, lafter = _along(lleft, lright, "mshort")
+    ltc, seen_c, gram, token = _core_prep(lext)
+    data, top, bot, left, right = _place(got, token)
+    before, after = _along(left, right, "mshort")
+    lpack = _pack(lbefore, lafter, ltop, lbot, right, True, "margin_left")
+    lhalos = (lbefore, lafter, *_along(*lpack, "mlong"))
     cross = _core_cross(data, seen_c, lext, ltc, right_factors)
-    lth, seen_h, inv = _inverse(gram, *lhalos)
-    back, new = _final(data, halos, seen_c, seen_h, lext, lhalos, lth, right_factors, cross, inv, got)
+    lth, seen_h, pred_h, part = _inverse_first(gram, *lhalos, right_factors, top)
+    pack = _pack(before, after, top, bot, lpack[0], False, "margin_data")
+    halos = (before, after, *_along(*pack, "mlong"))
+    inv = _inverse_second(part, pack[0])
+    back, new = _final(data, halos, seen_c, seen_h, lext, lth, pred_h, cross, inv, got)
     ret = _swap(back)
     new_right = _turn(new)
     return new_right, _give_back(ret, place)

time: 111 us -> 97.4 us (0.88)
  starting transfers between devices: 46.9 us -> 30.2 us
  waiting for transfers between devices: 27.1 us -> 35.6 us
  local copies, waits for them, and re-layouts: 6.21 us -> 2.72 us
  Pallas kernels: 29.2 us -> 27.6 us
    ppermute x4, starting transfers between devices: 13 us -> 2.37 us  [_along(): before = lax.ppermute(to_down, axis, fwd)]
    all_to_all x2, starting transfers between devices: 27.3 us -> 18.5 us  [_swap(): return lax.all_to_all(x, AXES, split_axis=0, concat_axis=0, tiled=True)]
    all_to_all x2, waiting for transfers between devices: 18.8 us -> 27.4 us  [_swap(): return lax.all_to_all(x, AXES, split_axis=0, concat_axis=0, tiled=True)]
    unnamed x42 -> x26, local copies, waits for them, and re-layouts: 6.21 us -> 2.72 us
    ppermute x4, starting transfers between devices: 6.61 us -> 9.24 us  [_along(): after = lax.ppermute(to_up, axis, [(j, i) for i, j in fwd])]
    ppermute x4, waiting for transfers between devices: 2.47 us -> 0.79 us  [_along(): after = lax.ppermute(to_up, axis, [(j, i) for i, j in fwd])]
    ppermute x4, waiting for transfers between devices: 5.84 us -> 7.44 us  [_along(): before = lax.ppermute(to_down, axis, fwd)]
    pallas_call x7 -> x8, Pallas kernels: 23.8 us -> 22.3 us  [the longest x1 5.26 us: _inverse_first(): pl.pallas_call(_inverse_first_body, in_specs=[_VMEM] * 6 + [_ANY], out_sh...]
  transfers between devices with their start and end apart: 10 -> 10, of which waited for: 5 -> 4; matrix products, arithmetic and copies ran while one was open for 0% -> 0% of each run, Pallas kernels for 13% -> 17%
where the time goes in v1:
time: 97.4 us; the launch traced here: 97.1 us
  waiting for transfers between devices  35.6 us (37%)
  starting transfers between devices  30.2 us (31%)
  Pallas kernels  27.6 us (28%)
  local copies, waits for them, and re-layouts  2.72 us (3%)
  between operations  1.02 us (1%)
    all_to_all x2, waiting for transfers between devices, _swap(): return lax.all_to_all(x, AXES, split_axis=0, concat_axis=0, tiled=True)  27.4 us
    all_to_all x2, starting transfers between devices, _swap(): return lax.all_to_all(x, AXES, split_axis=0, concat_axis=0, tiled=True)  18.5 us
    ppermute x4, starting transfers between devices, _along(): after = lax.ppermute(to_up, axis, [(j, i) for i, j in fwd])  9.24 us
    ppermute x4, waiting for transfers between devices, _along(): before = lax.ppermute(to_down, axis, fwd)  7.44 us
    pallas_call x1, Pallas kernels, _inverse_first(): pl.pallas_call(_inverse_first_body, in_specs=[_VMEM] * 6 + [_ANY], out_sh...  5.26 us
    pallas_call x1, Pallas kernels, _final(): pl.pallas_call(_final_body, in_specs=[_VMEM] * 13, out_specs=(_HBM, _VMEM...  5.23 us
    pallas_call x1, Pallas kernels, _inverse_second(): pl.pallas_call(_inverse_second_body, in_specs=[_VMEM, _ANY], out_shape=ja...  3.96 us
    pallas_call x1, Pallas kernels, _route(): pl.pallas_call(_route_body, in_specs=[_HBM] * 4, out_specs=(_HBM, _VMEM),...  3.69 us
  transfers between devices with their start and end apart: 10, of which 4 were waited for; matrix products, arithmetic and copies ran while one was open for 0% of the time, Pallas kernels for 17%

profile of v1, /device:TPU:1, one launch (start us, length us, event | category | flops | bytes accessed | tf_op | source)
XLA Modules:
  0.0 97.1 jit_solution(12200445248967599905)
XLA Ops:
  0.6 3.7 %route.1 = (bf16[1024,640]{1,0:T(8,128)(2,1)}, s32[512,128]{1,0:T(8,128)}) custom-call(s32[1,512]{1,0:T(1,128)} %bitcast.18, s32[1,512]{1,0:T(1,128)} %bitcast.19, s32[1,512]{1,0:T(1,128)} %bitcast.20, bf16[512,1024]{1,0:T(8,128)(2,1)} %tr_hbm.1), custom_call_target="tpu_custom_call" | custom-call | flops 1000000000 | bytes 4000000 | tf_op jit(solution)/shard_map/route/pallas_call | solution.py:133
  4.3 0.0 copy-start.11
  4.3 0.0 copy-start.10
  4.4 11.5 %all-to-all-start = ((bf16[128,8,640]{2,1,0:T(8,128)(2,1)}), bf16[128,8,640]{2,1,0:T(8,128)(2,1)S(1)}, u32[]{:S(2)}, u32[]{:S(2)}) async-start(bf16[128,8,640]{2,1,0:T(8,128)(2,1)} %bitcast.15), calls=%async_computation | async-start | bytes 2621440 | tf_op jit(solution)/shard_map/all_to_all | solution.py:557
  15.9 0.1 copy.9.bits_ref
  16.0 0.1 copy.12
  16.1 0.4 left_rows.1
  16.6 1.5 %collective-permute-start.2 = (bf16[64,640]{1,0:T(8,128)(2,1)S(1)}, bf16[64,640]{1,0:T(8,128)(2,1)S(1)}, u32[]{:S(2)}, u32[]{:S(2)}) collective-permute-start(bf16[64,640]{1,0:T(8,128)(2,1)S(1)} %get-tuple-element.36), channel_id=1, source_target_pairs={{0,1},{1,2},{2,3},{3,4},{4,5},{5,6},{6,7},{7,0},{8,9},{9,10},{10,1... | collective-permute-start | bytes 245768 | tf_op jit(solution)/shard_map/ppermute | solution.py:234
  18.0 4.1 %collective-permute-start.3 = (bf16[64,640]{1,0:T(8,128)(2,1)S(1)}, bf16[64,640]{1,0:T(8,128)(2,1)S(1)}, u32[]{:S(2)}, u32[]{:S(2)}) collective-permute-start(bf16[64,640]{1,0:T(8,128)(2,1)S(1)} %get-tuple-element.37), channel_id=1, source_target_pairs={{1,0},{2,1},{3,2},{4,3},{5,4},{6,5},{7,6},{0,7},{9,8},{10,9},{11,1... | collective-permute-start | bytes 245768 | tf_op jit(solution)/shard_map/ppermute | solution.py:235
  22.2 0.7 core_prep.1
  22.9 0.0 copy-start.3
  22.9 1.0 copy-done.3
  23.9 0.8 copy-done.6
  24.7 0.7 copy-done.8
  25.4 11.5 %all-to-all-done = bf16[128,8,640]{2,1,0:T(8,128)(2,1)S(1)} async-done(((bf16[128,8,640]{2,1,0:T(8,128)(2,1)}), bf16[128,8,640]{2,1,0:T(8,128)(2,1)S(1)}, u32[]{:S(2)}, u32[]{:S(2)}) %all-to-all-start) | async-done | bytes 1310752 | tf_op jit(solution)/shard_map/all_to_all | solution.py:557
  36.9 2.0 %to_grid.1 = (bf16[512,1152]{1,0:T(8,128)(2,1)S(1)}, bf16[128,1152]{1,0:T(8,128)(2,1)S(1)}, bf16[128,1152]{1,0:T(8,128)(2,1)S(1)}, bf16[64,1152]{1,0:T(8,128)(2,1)S(1)}, bf16[64,1152]{1,0:T(8,128)(2,1)S(1)}) custom-call(bf16[1024,640]{1,0:T(8,128)(2,1)S(1)} %bitcast.12, f32[8,128]{1,0:T(8,128)S(1)} %get-tuple-element.30.after_ref), custom_call_target="tpu_custom_call" | custom-call | flops 1000000000 | bytes 4000000 | tf_op jit(solution)/shard_map/to_grid/pallas_call | solution.py:190
  38.9 3.9 %collective-permute-start.1 = (bf16[64,1152]{1,0:T(8,128)(2,1)S(1)}, bf16[64,1152]{1,0:T(8,128)(2,1)S(1)}, u32[]{:S(2)}, u32[]{:S(2)}) collective-permute-start(bf16[64,1152]{1,0:T(8,128)(2,1)S(1)} %get-tuple-element.33), channel_id=1, source_target_pairs={{1,0},{2,1},{3,2},{4,3},{5,4},{6,5},{7,6},{0,7},{9,8},{10,9},{11,1... | collective-permute-start | bytes 442376 | tf_op jit(solution)/shard_map/ppermute | solution.py:235
  42.8 0.1 margin_left.1
  42.9 0.8 collective-permute-start.6
  43.8 1.9 %cross_core.1.cross_ref = f32[4,128,1024]{2,1,0:T(8,128)S(1)} custom-call(bf16[512,1152]{1,0:T(8,128)(2,1)S(1)} %get-tuple-element.31.data_ref, bf16[512,1024]{1,0:T(8,128)(2,1)S(1)} %copy-done.4, bf16[512,640]{1,0:T(8,128)(2,1)S(1)} %copy-done.2, bf16[4,128,512]{2,1,0:T(8,128)(2,1)S(1)} %copy-done.7, bf16[4,1024,128]{2,1,0:T(8,128)(2,1)S(1)} %copy-done), custom_call_target="tpu_custom_call" | custom-call | flops 3000000000 | bytes 6000000 | tf_op jit(solution)/shard_map/cross_core/pallas_call | solution.py:446
  45.7 0.8 collective-permute-done.1.after_ref
  46.4 7.4 %collective-permute-done.before_ref = bf16[64,1152]{1,0:T(8,128)(2,1)S(1)} collective-permute-done((bf16[64,1152]{1,0:T(8,128)(2,1)S(1)}, bf16[64,1152]{1,0:T(8,128)(2,1)S(1)}, u32[]{:S(2)}, u32[]{:S(2)}) %collective-permute-start) | collective-permute-done | bytes 147488 | tf_op jit(solution)/shard_map/ppermute | solution.py:234
  53.9 0.1 margin_data.1
  53.9 0.1 collective-permute-start.4
  54.0 1.2 %collective-permute-start.5 = (bf16[160,1152]{1,0:T(8,128)(2,1)S(1)}, bf16[160,1152]{1,0:T(8,128)(2,1)S(1)}, u32[]{:S(2)}, u32[]{:S(2)}) collective-permute-start(bf16[160,1152]{1,0:T(8,128)(2,1)S(1)} %get-tuple-element.42.token_ref), channel_id=1, source_target_pairs={{8,0},{16,8},{24,16},{32,24},{40,32},{48,40},{56,48},{64,56},{72,6... | collective-permute-start | bytes 1105928 | tf_op jit(solution)/shard_map/ppermute | solution.py:235
  55.2 5.3 %inverse_first.1 = (bf16[4,128,448]{2,1,0:T(8,128)(2,1)S(1)}, bf16[448,1024]{1,0:T(8,128)(2,1)S(1)}, bf16[4,448,1024]{2,1,0:T(8,128)(2,1)S(1)}, f32[4,128,128]{2,1,0:T(8,128)S(1)}) custom-call(f32[4,128,128]{2,1,0:T(8,128)S(1)} %copy-done.9, bf16[64,640]{1,0:T(8,128)(2,1)S(1)} %collective-permute-done.2.before_ref, ...), custom_call_target="tpu_custom_call" | custom-call | flops 4000000000 | bytes 4000000 | tf_op jit(solution)/shard_map/inverse_first/pallas_call | solution.py:396
  60.5 4.0 %inverse_second.1.inv_ref = f32[4,128,128]{2,1,0:T(8,128)S(1)} custom-call(f32[4,128,128]{2,1,0:T(8,128)S(1)} %get-tuple-element.50.part_ref, bf16[160,1152]{1,0:T(8,128)(2,1)S(1)} %get-tuple-element.42.token_ref), custom_call_target="tpu_custom_call" | custom-call | flops 4000000000 | bytes 1000000 | tf_op jit(solution)/shard_map/inverse_second/pallas_call | solution.py:417
  64.5 5.2 %update_residual.1 = (bf16[1024,512]{1,0:T(8,128)(2,1)}, f32[4,128,1024]{2,1,0:T(8,128)S(1)}) custom-call(bf16[512,1152]{1,0:T(8,128)(2,1)S(1)} %get-tuple-element.31.data_ref, bf16[64,1152]{1,0:T(8,128)(2,1)S(1)} %collective-permute-done.before_ref, bf16[64,1152]{1,0:T(8,128)(2,1)S(1)} %collective-permute-done.1.after_ref, ...), custom_call_target="tpu_custom_call" | custom-call | flops 4000000000 | bytes 10000000 | tf_op jit(solution)/shard_map/update_residual/pallas_call | solution.py:495
  69.7 7.0 %all-to-all-start.1 = ((bf16[128,8,512]{2,1,0:T(8,128)(2,1)}), bf16[128,8,512]{2,1,0:T(8,128)(2,1)S(1)}, u32[]{:S(2)}, u32[]{:S(2)}) async-start(bf16[128,8,512]{2,1,0:T(8,128)(2,1)} %bitcast.16), calls=%async_computation.1 | async-start | bytes 2097152 | tf_op jit(solution)/shard_map/all_to_all | solution.py:557
  76.8 2.2 %new_right.1 = f32[4,1024,128]{2,1,0:T(8,128)} custom-call(f32[4,128,1024]{2,1,0:T(8,128)S(1)} %get-tuple-element.51.new_ref), custom_call_target="tpu_custom_call" | custom-call | flops 1000000 | bytes 4000000 | tf_op jit(solution)/shard_map/new_right/pallas_call | solution.py:515
  79.0 15.9 %all-to-all-done.1 = bf16[128,8,512]{2,1,0:T(8,128)(2,1)S(1)} async-done(((bf16[128,8,512]{2,1,0:T(8,128)(2,1)}), bf16[128,8,512]{2,1,0:T(8,128)(2,1)S(1)}, u32[]{:S(2)}, u32[]{:S(2)}) %all-to-all-start.1) | async-done | bytes 1048608 | tf_op jit(solution)/shard_map/all_to_all | solution.py:557
  94.9 2.0 %give_back.1 = bf16[512,1024]{1,0:T(8,128)(2,1)} custom-call(bf16[1024,512]{1,0:T(8,128)(2,1)S(1)} %bitcast.14, s32[512,128]{1,0:T(8,128)S(1)} %copy-done.5), custom_call_target="tpu_custom_call" | custom-call | flops 1000000000 | bytes 4000000 | tf_op jit(solution)/shard_map/give_back/pallas_call | solution.py:544
  (26 shorter events, 0.1 us)
Async XLA Ops:
  4.3 11.5 %copy-start.11 = (s32[512,64]{0,1:T(8,128)S(1)}, s32[512,64]{0,1:T(8,128)}, u32[]{:S(2)}) copy-start(s32[512,64]{0,1:T(8,128)} %param.11) | copy-start | bytes 393220
  4.3 11.7 %copy-start.10 = (bf16[512,4,128]{2,1,0:T(4,128)(2,1)S(1)}, bf16[512,4,128]{2,1,0:T(4,128)(2,1)}, u32[]{:S(2)}) copy-start(bf16[512,4,128]{2,1,0:T(4,128)(2,1)} %param.12) | copy-start | bytes 1572868
  4.4 32.5 %all-to-all-start = ((bf16[128,8,640]{2,1,0:T(8,128)(2,1)}), bf16[128,8,640]{2,1,0:T(8,128)(2,1)S(1)}, u32[]{:S(2)}, u32[]{:S(2)}) async-start(bf16[128,8,640]{2,1,0:T(8,128)(2,1)} %bitcast.15), calls=%async_computation | async-start | bytes 2621440 | tf_op jit(solution)/shard_map/all_to_all | solution.py:557
  16.5 20.3 %copy-start.1 = (bf16[512,640]{1,0:T(8,128)(2,1)}, bf16[512,640]{1,0:T(8,128)(2,1)S(1)}, u32[]{:S(2)}) copy-start(bf16[512,640]{1,0:T(8,128)(2,1)S(1)} %get-tuple-element.29.core_ref.l_ref.lc_ref) | copy-start | bytes 1966084
  16.6 26.2 %collective-permute-start.2 = (bf16[64,640]{1,0:T(8,128)(2,1)S(1)}, bf16[64,640]{1,0:T(8,128)(2,1)S(1)}, u32[]{:S(2)}, u32[]{:S(2)}) collective-permute-start(bf16[64,640]{1,0:T(8,128)(2,1)S(1)} %get-tuple-element.36), channel_id=1, source_target_pairs={{0,1},{1,2},{2,3},{3,4},{4,5},{5,6},{6,7},{7,0},{8,9},{9,10},{10,1... | collective-permute-start | bytes 245768 | tf_op jit(solution)/shard_map/ppermute | solution.py:234
  18.0 24.8 %collective-permute-start.3 = (bf16[64,640]{1,0:T(8,128)(2,1)S(1)}, bf16[64,640]{1,0:T(8,128)(2,1)S(1)}, u32[]{:S(2)}, u32[]{:S(2)}) collective-permute-start(bf16[64,640]{1,0:T(8,128)(2,1)S(1)} %get-tuple-element.37), channel_id=1, source_target_pairs={{1,0},{2,1},{3,2},{4,3},{5,4},{6,5},{7,6},{0,7},{9,8},{10,9},{11,1... | collective-permute-start | bytes 245768 | tf_op jit(solution)/shard_map/ppermute | solution.py:235
  22.9 1.0 %copy-start.3 = (bf16[512,1024]{1,0:T(8,128)(2,1)}, bf16[512,1024]{1,0:T(8,128)(2,1)S(1)}, u32[]{:S(2)}) copy-start(bf16[512,1024]{1,0:T(8,128)(2,1)S(1)} %get-tuple-element.43.seen_ref.seen_c_ref) | copy-start | bytes 3145732
  23.9 0.8 copy-start.6
  24.7 0.7 copy-start.8
  36.9 6.9 %copy-start = (bf16[4,1024,128]{2,1,0:T(8,128)(2,1)S(1)}, bf16[4,1024,128]{2,1,0:T(8,128)(2,1)}, u32[]{:S(2)}) copy-start(bf16[4,1024,128]{2,1,0:T(8,128)(2,1)} %v_ref.3) | copy-start | bytes 3145732
  36.9 6.9 %copy-start.2 = (bf16[512,640]{1,0:T(8,128)(2,1)S(1)}, bf16[512,640]{1,0:T(8,128)(2,1)}, u32[]{:S(2)}) copy-start(bf16[512,640]{1,0:T(8,128)(2,1)} %copy-done.1) | copy-start | bytes 1966084
  36.9 6.9 %copy-start.4 = (bf16[512,1024]{1,0:T(8,128)(2,1)S(1)}, bf16[512,1024]{1,0:T(8,128)(2,1)}, u32[]{:S(2)}) copy-start(bf16[512,1024]{1,0:T(8,128)(2,1)} %copy-done.3) | copy-start | bytes 3145732
  36.9 6.9 %copy-start.7 = (bf16[4,128,512]{2,1,0:T(8,128)(2,1)S(1)}, bf16[4,128,512]{2,1,0:T(8,128)(2,1)}, u32[]{:S(2)}) copy-start(bf16[4,128,512]{2,1,0:T(8,128)(2,1)} %copy-done.6) | copy-start | bytes 1572868
  38.9 7.5 %collective-permute-start.1 = (bf16[64,1152]{1,0:T(8,128)(2,1)S(1)}, bf16[64,1152]{1,0:T(8,128)(2,1)S(1)}, u32[]{:S(2)}, u32[]{:S(2)}) collective-permute-start(bf16[64,1152]{1,0:T(8,128)(2,1)S(1)} %get-tuple-element.33), channel_id=1, source_target_pairs={{1,0},{2,1},{3,2},{4,3},{5,4},{6,5},{7,6},{0,7},{9,8},{10,9},{11,1... | collective-permute-start | bytes 442376 | tf_op jit(solution)/shard_map/ppermute | solution.py:235
  42.8 11.1 %collective-permute-start = (bf16[64,1152]{1,0:T(8,128)(2,1)S(1)}, bf16[64,1152]{1,0:T(8,128)(2,1)S(1)}, u32[]{:S(2)}, u32[]{:S(2)}) collective-permute-start(bf16[64,1152]{1,0:T(8,128)(2,1)S(1)} %get-tuple-element.32.token_ref), channel_id=1, source_target_pairs={{0,1},{1,2},{2,3},{3,4},{4,5},{5,6},{6,7},{7,0},{8,9},{9,10},{10,1... | collective-permute-start | bytes 442376 | tf_op jit(solution)/shard_map/ppermute | solution.py:234
  42.9 12.4 %collective-permute-start.6 = (bf16[160,640]{1,0:T(8,128)(2,1)S(1)}, bf16[160,640]{1,0:T(8,128)(2,1)S(1)}, u32[]{:S(2)}, u32[]{:S(2)}) collective-permute-start(bf16[160,640]{1,0:T(8,128)(2,1)S(1)} %get-tuple-element.45), channel_id=1, source_target_pairs={{0,8},{8,16},{16,24},{24,32},{32,40},{40,48},{48,56},{56,64},{64,7... | collective-permute-start | bytes 614408 | tf_op jit(solution)/shard_map/ppermute | solution.py:234
  43.7 11.5 %collective-permute-start.7 = (bf16[160,640]{1,0:T(8,128)(2,1)S(1)}, bf16[160,640]{1,0:T(8,128)(2,1)S(1)}, u32[]{:S(2)}, u32[]{:S(2)}) collective-permute-start(bf16[160,640]{1,0:T(8,128)(2,1)S(1)} %get-tuple-element.40.token_ref), channel_id=1, source_target_pairs={{8,0},{16,8},{24,16},{32,24},{40,32},{48,40},{56,48},{64,56},{72,6... | collective-permute-start | bytes 614408 | tf_op jit(solution)/shard_map/ppermute | solution.py:235
  43.8 11.5 %copy-start.9 = (f32[4,128,128]{2,1,0:T(8,128)S(1)}, f32[4,128,128]{2,1,0:T(8,128)}, u32[]{:S(2)}) copy-start(f32[4,128,128]{2,1,0:T(8,128)} %copy-done.8) | copy-start | bytes 786436
  53.9 10.6 %collective-permute-start.4 = (bf16[160,1152]{1,0:T(8,128)(2,1)S(1)}, bf16[160,1152]{1,0:T(8,128)(2,1)S(1)}, u32[]{:S(2)}, u32[]{:S(2)}) collective-permute-start(bf16[160,1152]{1,0:T(8,128)(2,1)S(1)} %get-tuple-element.41), channel_id=1, source_target_pairs={{0,8},{8,16},{16,24},{24,32},{32,40},{40,48},{48,56},{56,64},{64,7... | collective-permute-start | bytes 1105928 | tf_op jit(solution)/shard_map/ppermute | solution.py:234
  54.0 10.5 %collective-permute-start.5 = (bf16[160,1152]{1,0:T(8,128)(2,1)S(1)}, bf16[160,1152]{1,0:T(8,128)(2,1)S(1)}, u32[]{:S(2)}, u32[]{:S(2)}) collective-permute-start(bf16[160,1152]{1,0:T(8,128)(2,1)S(1)} %get-tuple-element.42.token_ref), channel_id=1, source_target_pairs={{8,0},{16,8},{24,16},{32,24},{40,32},{48,40},{56,48},{64,56},{72,6... | collective-permute-start | bytes 1105928 | tf_op jit(solution)/shard_map/ppermute | solution.py:235
  69.7 25.2 %all-to-all-start.1 = ((bf16[128,8,512]{2,1,0:T(8,128)(2,1)}), bf16[128,8,512]{2,1,0:T(8,128)(2,1)S(1)}, u32[]{:S(2)}, u32[]{:S(2)}) async-start(bf16[128,8,512]{2,1,0:T(8,128)(2,1)} %bitcast.16), calls=%async_computation.1 | async-start | bytes 2097152 | tf_op jit(solution)/shard_map/all_to_all | solution.py:557
  76.8 18.1 %copy-start.5 = (s32[512,128]{1,0:T(8,128)S(1)}, s32[512,128]{1,0:T(8,128)}, u32[]{:S(2)}) copy-start(s32[512,128]{1,0:T(8,128)} %get-tuple-element.53.place_ref) | copy-start | bytes 786436

commit v2 on v1

--- a/solution.py
+++ b/solution.py
@@ -68,6 +68,12 @@
     even = jnp.concatenate([left[:, :CAP], right[:, :CAP]], axis=1)
     odd = jnp.concatenate([left[:, CAP:], right[:, CAP:]], axis=1)
     return jnp.stack([even, odd], axis=1).reshape(-1, HALF)
+
+
+def _unweave(x):
+    t = x.reshape(x.shape[0] // (2 * SLOT), 2, SLOT, x.shape[1])
+    join = lambda rows: jnp.concatenate([t[:, 0, rows], t[:, 1, rows]], axis=1).reshape(-1, x.shape[1])
+    return join(slice(0, CAP)), join(slice(CAP, SLOT))
 
 
 def _side_select(shape, first):
@@ -107,9 +113,7 @@
     cs = _iota((ROWS, ROWS), 1)
     within = jnp.sum(jnp.where(same & (rs < cs), 1.0, 0.0), axis=0, keepdims=True)
     place = jnp.where(valid, ownf * CAP + within, -64.0).astype(jnp.int32)
-    within_c = jnp.sum(jnp.where(same & (cs < rs), 1.0, 0.0), axis=1, keepdims=True)
-    place_c = jnp.where(ocol >= 0.0, ocol * SLOT + within_c, -64.0)
-    place_ref[...] = jnp.broadcast_to(place_c, (ROWS, LANE)).astype(jnp.int32)
+    place_ref[...] = jnp.broadcast_to(place.astype(F32), (LANE, ROWS)).T.astype(jnp.int32)
     meta_b = meta_t.astype(BF)
     load.wait()
     step = 128
@@ -158,19 +162,16 @@
 
 
 def _place_body(got_ref, after_ref, core_ref, top_ref, bot_ref, left_ref, right_ref):
-    meta = got_ref[:, HALF:].astype(F32).T
+    notes = _unweave(got_ref[:, HALF:].astype(F32))[0]
+    meta = notes.T
+    notes = notes.astype(BF)
     m = _slot_rows((meta[0:1], meta[1:2], meta[2:3]))
-    half = (_iota((1, NSLOT), 1) // CAP) % 2
-    m0 = jnp.where(half == 0, m, -1)
-    m1 = jnp.where(half == 1, m, -1)
+    traces = jnp.concatenate(_unweave(got_ref[:, :HALF].astype(F32)), axis=1).astype(BF)
     step = 128
     for base in range(0, ROWS, step):
-        r = _iota((step, NSLOT), 0) + base
-        hot0 = _hot(r == m0)
-        hot1 = _hot(r == m1)
-        d0 = _dot(hot0, got_ref[:, :HALF]).astype(BF)
-        d1 = _dot(hot1, got_ref[:, :HALF]).astype(BF)
-        f = _dot(hot0, got_ref[:, HALF:])[:, 3:4]
+        hot = _hot(_iota((step, ROWS), 0) + base == m)
+        d = _dot(hot, traces).astype(BF)
+        f = _dot(hot, notes)[:, 3:4]
         f = jnp.broadcast_to(f, (step, LANE)).astype(BF)
         spots = [(core_ref, base)]
         if base == 0:
@@ -178,8 +179,7 @@
         if base == ROWS - STRIP:
             spots.append((bot_ref, 0))
         for ref, at in spots:
-            ref[at : at + step, :HALF] = d0
-            ref[at : at + step, HALF:W] = d1
+            ref[at : at + step, :W] = d
             ref[at : at + step, W:] = f
     core = core_ref[...]
     left_ref[...] = _dot(_side_select((SIDE, ROWS), 0), core).astype(BF)
@@ -289,6 +289,13 @@
     left = jnp.concatenate([ah, ah, am, ah, am, al], axis=0)
     right = jnp.concatenate([bh, bm, bh, bl, bm, bh], axis=0)
     return lax.dot_general(left, right, (((0,), (0,)), ((), ())), preferred_element_type=F32)
+
+
+def _dot6(a, b):
+    ah, am, al = _split3(a)
+    bh, bm, bl = _split3(b)
+    left = jnp.concatenate([ah, ah, am, ah, am, al], axis=1)
+    return _dot(left, jnp.concatenate([bh, bm, bh, bl, bm, bh], axis=0))
 
 
 def _eliminate(g_ref, first, last):
@@ -464,7 +471,7 @@
     for f in range(FOLDS):
         fill = _fill(seen_h_ref[...], _threshold(foldp, f), halo, pred_ref[f])
         cross = cross_ref[f] + _dot(lth_ref[f], fill)
-        new_ref[f] = jnp.dot(inv_ref[f], cross, preferred_element_type=F32, precision=lax.Precision.HIGHEST)
+        new_ref[f] = _dot6(inv_ref[f], cross)
     lsel = []
     news = []
     for f in range(FOLDS):
@@ -525,14 +532,12 @@
 
 
 def _return_body(ret_ref, place_ref, out_hbm, out_ref, sem):
+    ret = jnp.concatenate(_unweave(ret_ref[...].astype(F32)), axis=1).astype(BF)
     step = 128
     stores = []
     for i, base in enumerate(range(0, ROWS, step)):
         out = slice(base, base + step)
-        place = place_ref[out, :1]
-        r = _iota((step, NSLOT), 1)
-        out_ref[out, :HALF] = _dot(_hot(r == place), ret_ref[...]).astype(BF)
-        out_ref[out, HALF:] = _dot(_hot(r == place + CAP), ret_ref[...]).astype(BF)
+        out_ref[out, :] = _dot(_hot(_iota((step, ROWS), 1) == place_ref[out, :1]), ret).astype(BF)
         store = pltpu.make_async_copy(out_ref.at[out], out_hbm.at[out], sem.at[i])
         store.start()
         stores.append(store)

time: 97.4 us -> 96 us (0.986)
  Pallas kernels: 27.6 us -> 26.2 us
where the time goes in v2:
time: 96 us; the launch traced here: 95.7 us
  waiting for transfers between devices  35.6 us (37%)
  starting transfers between devices  30.2 us (31%)
  Pallas kernels  26.2 us (27%)
  local copies, waits for them, and re-layouts  2.72 us (3%)
  between operations  1.02 us (1%)
    all_to_all x2, waiting for transfers between devices, _swap(): return lax.all_to_all(x, AXES, split_axis=0, concat_axis=0, tiled=True)  27.4 us
    all_to_all x2, starting transfers between devices, _swap(): return lax.all_to_all(x, AXES, split_axis=0, concat_axis=0, tiled=True)  18.6 us
    ppermute x4, starting transfers between devices, _along(): after = lax.ppermute(to_up, axis, [(j, i) for i, j in fwd])  9.25 us
    ppermute x4, waiting for transfers between devices, _along(): before = lax.ppermute(to_down, axis, fwd)  7.44 us
    pallas_call x1, Pallas kernels, _inverse_first(): pl.pallas_call(_inverse_first_body, in_specs=[_VMEM] * 6 + [_ANY], out_sh...  5.26 us
    pallas_call x1, Pallas kernels, _final(): pl.pallas_call(_final_body, in_specs=[_VMEM] * 13, out_specs=(_HBM, _VMEM...  4.6 us
    pallas_call x1, Pallas kernels, _inverse_second(): pl.pallas_call(_inverse_second_body, in_specs=[_VMEM, _ANY], out_shape=ja...  3.96 us
    pallas_call x1, Pallas kernels, _route(): pl.pallas_call(_route_body, in_specs=[_HBM] * 4, out_specs=(_HBM, _VMEM),...  3.7 us
  transfers between devices with their start and end apart: 10, of which 4 were waited for; matrix products, arithmetic and copies ran while one was open for 0% of the time, Pallas kernels for 17%

profile of v2, /device:TPU:1, one launch (start us, length us, event | category | flops | bytes accessed | tf_op | source)
XLA Modules:
  0.0 95.7 jit_solution(8704443124030097654)
XLA Ops:
  0.6 3.7 %route.1 = (bf16[1024,640]{1,0:T(8,128)(2,1)}, s32[512,128]{1,0:T(8,128)}) custom-call(s32[1,512]{1,0:T(1,128)} %bitcast.18, s32[1,512]{1,0:T(1,128)} %bitcast.19, s32[1,512]{1,0:T(1,128)} %bitcast.20, bf16[512,1024]{1,0:T(8,128)(2,1)} %tr_hbm.1), custom_call_target="tpu_custom_call" | custom-call | flops 1000000000 | bytes 4000000 | tf_op jit(solution)/shard_map/route/pallas_call | solution.py:137
  4.3 0.0 copy-start.11
  4.3 0.0 copy-start.10
  4.4 11.5 %all-to-all-start = ((bf16[128,8,640]{2,1,0:T(8,128)(2,1)}), bf16[128,8,640]{2,1,0:T(8,128)(2,1)S(1)}, u32[]{:S(2)}, u32[]{:S(2)}) async-start(bf16[128,8,640]{2,1,0:T(8,128)(2,1)} %bitcast.15), calls=%async_computation | async-start | bytes 2621440 | tf_op jit(solution)/shard_map/all_to_all | solution.py:562
  15.9 0.1 copy.9.bits_ref
  16.0 0.1 copy.12
  16.1 0.4 left_rows.1
  16.6 1.5 %collective-permute-start.2 = (bf16[64,640]{1,0:T(8,128)(2,1)S(1)}, bf16[64,640]{1,0:T(8,128)(2,1)S(1)}, u32[]{:S(2)}, u32[]{:S(2)}) collective-permute-start(bf16[64,640]{1,0:T(8,128)(2,1)S(1)} %get-tuple-element.36), channel_id=1, source_target_pairs={{0,1},{1,2},{2,3},{3,4},{4,5},{5,6},{6,7},{7,0},{8,9},{9,10},{10,1... | collective-permute-start | bytes 245768 | tf_op jit(solution)/shard_map/ppermute | solution.py:234
  18.0 4.1 %collective-permute-start.3 = (bf16[64,640]{1,0:T(8,128)(2,1)S(1)}, bf16[64,640]{1,0:T(8,128)(2,1)S(1)}, u32[]{:S(2)}, u32[]{:S(2)}) collective-permute-start(bf16[64,640]{1,0:T(8,128)(2,1)S(1)} %get-tuple-element.37), channel_id=1, source_target_pairs={{1,0},{2,1},{3,2},{4,3},{5,4},{6,5},{7,6},{0,7},{9,8},{10,9},{11,1... | collective-permute-start | bytes 245768 | tf_op jit(solution)/shard_map/ppermute | solution.py:235
  22.2 0.7 core_prep.1
  22.9 0.0 copy-start.3
  22.9 1.0 %copy-done.3 = bf16[512,1024]{1,0:T(8,128)(2,1)} copy-done((bf16[512,1024]{1,0:T(8,128)(2,1)}, bf16[512,1024]{1,0:T(8,128)(2,1)S(1)}, u32[]{:S(2)}) %copy-start.3) | copy-done | bytes 1048600
  23.9 0.8 copy-done.6
  24.7 0.7 copy-done.8
  25.4 11.5 %all-to-all-done = bf16[128,8,640]{2,1,0:T(8,128)(2,1)S(1)} async-done(((bf16[128,8,640]{2,1,0:T(8,128)(2,1)}), bf16[128,8,640]{2,1,0:T(8,128)(2,1)S(1)}, u32[]{:S(2)}, u32[]{:S(2)}) %all-to-all-start) | async-done | bytes 1310752 | tf_op jit(solution)/shard_map/all_to_all | solution.py:562
  36.9 1.5 %to_grid.1 = (bf16[512,1152]{1,0:T(8,128)(2,1)S(1)}, bf16[128,1152]{1,0:T(8,128)(2,1)S(1)}, bf16[128,1152]{1,0:T(8,128)(2,1)S(1)}, bf16[64,1152]{1,0:T(8,128)(2,1)S(1)}, bf16[64,1152]{1,0:T(8,128)(2,1)S(1)}) custom-call(bf16[1024,640]{1,0:T(8,128)(2,1)S(1)} %bitcast.12, f32[8,128]{1,0:T(8,128)S(1)} %get-tuple-element.30.after_ref), custom_call_target="tpu_custom_call" | custom-call | flops 1000000000 | bytes 4000000 | tf_op jit(solution)/shard_map/to_grid/pallas_call | solution.py:190
  38.4 3.9 %collective-permute-start.1 = (bf16[64,1152]{1,0:T(8,128)(2,1)S(1)}, bf16[64,1152]{1,0:T(8,128)(2,1)S(1)}, u32[]{:S(2)}, u32[]{:S(2)}) collective-permute-start(bf16[64,1152]{1,0:T(8,128)(2,1)S(1)} %get-tuple-element.33), channel_id=1, source_target_pairs={{1,0},{2,1},{3,2},{4,3},{5,4},{6,5},{7,6},{0,7},{9,8},{10,9},{11,1... | collective-permute-start | bytes 442376 | tf_op jit(solution)/shard_map/ppermute | solution.py:235
  42.3 0.1 margin_left.1
  42.4 0.8 collective-permute-start.6
  43.3 1.9 %cross_core.1.cross_ref = f32[4,128,1024]{2,1,0:T(8,128)S(1)} custom-call(bf16[512,1152]{1,0:T(8,128)(2,1)S(1)} %get-tuple-element.31.data_ref, bf16[512,1024]{1,0:T(8,128)(2,1)S(1)} %copy-done.4, bf16[512,640]{1,0:T(8,128)(2,1)S(1)} %copy-done.2, bf16[4,128,512]{2,1,0:T(8,128)(2,1)S(1)} %copy-done.7, bf16[4,1024,128]{2,1,0:T(8,128)(2,1)S(1)} %copy-done), custom_call_target="tpu_custom_call" | custom-call | flops 3000000000 | bytes 6000000 | tf_op jit(solution)/shard_map/cross_core/pallas_call | solution.py:453
  45.2 0.8 collective-permute-done.1.after_ref
  46.0 7.4 %collective-permute-done.before_ref = bf16[64,1152]{1,0:T(8,128)(2,1)S(1)} collective-permute-done((bf16[64,1152]{1,0:T(8,128)(2,1)S(1)}, bf16[64,1152]{1,0:T(8,128)(2,1)S(1)}, u32[]{:S(2)}, u32[]{:S(2)}) %collective-permute-start) | collective-permute-done | bytes 147488 | tf_op jit(solution)/shard_map/ppermute | solution.py:234
  53.4 0.1 margin_data.1
  53.5 0.1 collective-permute-start.4
  53.6 1.2 %collective-permute-start.5 = (bf16[160,1152]{1,0:T(8,128)(2,1)S(1)}, bf16[160,1152]{1,0:T(8,128)(2,1)S(1)}, u32[]{:S(2)}, u32[]{:S(2)}) collective-permute-start(bf16[160,1152]{1,0:T(8,128)(2,1)S(1)} %get-tuple-element.42.token_ref), channel_id=1, source_target_pairs={{8,0},{16,8},{24,16},{32,24},{40,32},{48,40},{56,48},{64,56},{72,6... | collective-permute-start | bytes 1105928 | tf_op jit(solution)/shard_map/ppermute | solution.py:235
  54.8 5.3 %inverse_first.1 = (bf16[4,128,448]{2,1,0:T(8,128)(2,1)S(1)}, bf16[448,1024]{1,0:T(8,128)(2,1)S(1)}, bf16[4,448,1024]{2,1,0:T(8,128)(2,1)S(1)}, f32[4,128,128]{2,1,0:T(8,128)S(1)}) custom-call(f32[4,128,128]{2,1,0:T(8,128)S(1)} %copy-done.9, bf16[64,640]{1,0:T(8,128)(2,1)S(1)} %collective-permute-done.2.before_ref, ...), custom_call_target="tpu_custom_call" | custom-call | flops 4000000000 | bytes 4000000 | tf_op jit(solution)/shard_map/inverse_first/pallas_call | solution.py:403
  60.1 4.0 %inverse_second.1.inv_ref = f32[4,128,128]{2,1,0:T(8,128)S(1)} custom-call(f32[4,128,128]{2,1,0:T(8,128)S(1)} %get-tuple-element.50.part_ref, bf16[160,1152]{1,0:T(8,128)(2,1)S(1)} %get-tuple-element.42.token_ref), custom_call_target="tpu_custom_call" | custom-call | flops 4000000000 | bytes 1000000 | tf_op jit(solution)/shard_map/inverse_second/pallas_call | solution.py:424
  64.0 4.6 %update_residual.1 = (bf16[1024,512]{1,0:T(8,128)(2,1)}, f32[4,128,1024]{2,1,0:T(8,128)S(1)}) custom-call(bf16[512,1152]{1,0:T(8,128)(2,1)S(1)} %get-tuple-element.31.data_ref, bf16[64,1152]{1,0:T(8,128)(2,1)S(1)} %collective-permute-done.before_ref, bf16[64,1152]{1,0:T(8,128)(2,1)S(1)} %collective-permute-done.1.after_ref, ...), custom_call_target="tpu_custom_call" | custom-call | flops 4000000000 | bytes 10000000 | tf_op jit(solution)/shard_map/update_residual/pallas_call | solution.py:502
  68.7 7.1 %all-to-all-start.1 = ((bf16[128,8,512]{2,1,0:T(8,128)(2,1)}), bf16[128,8,512]{2,1,0:T(8,128)(2,1)S(1)}, u32[]{:S(2)}, u32[]{:S(2)}) async-start(bf16[128,8,512]{2,1,0:T(8,128)(2,1)} %bitcast.16), calls=%async_computation.1 | async-start | bytes 2097152 | tf_op jit(solution)/shard_map/all_to_all | solution.py:562
  75.7 2.2 %new_right.1 = f32[4,1024,128]{2,1,0:T(8,128)} custom-call(f32[4,128,1024]{2,1,0:T(8,128)S(1)} %get-tuple-element.51.new_ref), custom_call_target="tpu_custom_call" | custom-call | flops 1000000 | bytes 4000000 | tf_op jit(solution)/shard_map/new_right/pallas_call | solution.py:522
  78.0 15.9 %all-to-all-done.1 = bf16[128,8,512]{2,1,0:T(8,128)(2,1)S(1)} async-done(((bf16[128,8,512]{2,1,0:T(8,128)(2,1)}), bf16[128,8,512]{2,1,0:T(8,128)(2,1)S(1)}, u32[]{:S(2)}, u32[]{:S(2)}) %all-to-all-start.1) | async-done | bytes 1048608 | tf_op jit(solution)/shard_map/all_to_all | solution.py:562
  93.9 1.7 %give_back.1 = bf16[512,1024]{1,0:T(8,128)(2,1)} custom-call(bf16[1024,512]{1,0:T(8,128)(2,1)S(1)} %bitcast.14, s32[512,128]{1,0:T(8,128)S(1)} %copy-done.5), custom_call_target="tpu_custom_call" | custom-call | flops 1000000000 | bytes 4000000 | tf_op jit(solution)/shard_map/give_back/pallas_call | solution.py:549
  (26 shorter events, 0.1 us)
Async XLA Ops:
  4.3 11.5 %copy-start.11 = (s32[512,64]{0,1:T(8,128)S(1)}, s32[512,64]{0,1:T(8,128)}, u32[]{:S(2)}) copy-start(s32[512,64]{0,1:T(8,128)} %param.11) | copy-start | bytes 393220
  4.3 11.7 %copy-start.10 = (bf16[512,4,128]{2,1,0:T(4,128)(2,1)S(1)}, bf16[512,4,128]{2,1,0:T(4,128)(2,1)}, u32[]{:S(2)}) copy-start(bf16[512,4,128]{2,1,0:T(4,128)(2,1)} %param.12) | copy-start | bytes 1572868
  4.4 32.5 %all-to-all-start = ((bf16[128,8,640]{2,1,0:T(8,128)(2,1)}), bf16[128,8,640]{2,1,0:T(8,128)(2,1)S(1)}, u32[]{:S(2)}, u32[]{:S(2)}) async-start(bf16[128,8,640]{2,1,0:T(8,128)(2,1)} %bitcast.15), calls=%async_computation | async-start | bytes 2621440 | tf_op jit(solution)/shard_map/all_to_all | solution.py:562
  16.5 20.3 %copy-start.1 = (bf16[512,640]{1,0:T(8,128)(2,1)}, bf16[512,640]{1,0:T(8,128)(2,1)S(1)}, u32[]{:S(2)}) copy-start(bf16[512,640]{1,0:T(8,128)(2,1)S(1)} %get-tuple-element.29.core_ref.l_ref.lc_ref) | copy-start | bytes 1966084
  16.6 25.8 %collective-permute-start.2 = (bf16[64,640]{1,0:T(8,128)(2,1)S(1)}, bf16[64,640]{1,0:T(8,128)(2,1)S(1)}, u32[]{:S(2)}, u32[]{:S(2)}) collective-permute-start(bf16[64,640]{1,0:T(8,128)(2,1)S(1)} %get-tuple-element.36), channel_id=1, source_target_pairs={{0,1},{1,2},{2,3},{3,4},{4,5},{5,6},{6,7},{7,0},{8,9},{9,10},{10,1... | collective-permute-start | bytes 245768 | tf_op jit(solution)/shard_map/ppermute | solution.py:234
  18.0 24.3 %collective-permute-start.3 = (bf16[64,640]{1,0:T(8,128)(2,1)S(1)}, bf16[64,640]{1,0:T(8,128)(2,1)S(1)}, u32[]{:S(2)}, u32[]{:S(2)}) collective-permute-start(bf16[64,640]{1,0:T(8,128)(2,1)S(1)} %get-tuple-element.37), channel_id=1, source_target_pairs={{1,0},{2,1},{3,2},{4,3},{5,4},{6,5},{7,6},{0,7},{9,8},{10,9},{11,1... | collective-permute-start | bytes 245768 | tf_op jit(solution)/shard_map/ppermute | solution.py:235
  22.9 1.0 %copy-start.3 = (bf16[512,1024]{1,0:T(8,128)(2,1)}, bf16[512,1024]{1,0:T(8,128)(2,1)S(1)}, u32[]{:S(2)}) copy-start(bf16[512,1024]{1,0:T(8,128)(2,1)S(1)} %get-tuple-element.43.seen_ref.seen_c_ref) | copy-start | bytes 3145732
  23.9 0.8 copy-start.6
  24.7 0.7 copy-start.8
  36.9 6.4 %copy-start = (bf16[4,1024,128]{2,1,0:T(8,128)(2,1)S(1)}, bf16[4,1024,128]{2,1,0:T(8,128)(2,1)}, u32[]{:S(2)}) copy-start(bf16[4,1024,128]{2,1,0:T(8,128)(2,1)} %v_ref.3) | copy-start | bytes 3145732
  36.9 6.4 %copy-start.2 = (bf16[512,640]{1,0:T(8,128)(2,1)S(1)}, bf16[512,640]{1,0:T(8,128)(2,1)}, u32[]{:S(2)}) copy-start(bf16[512,640]{1,0:T(8,128)(2,1)} %copy-done.1) | copy-start | bytes 1966084
  36.9 6.4 %copy-start.4 = (bf16[512,1024]{1,0:T(8,128)(2,1)S(1)}, bf16[512,1024]{1,0:T(8,128)(2,1)}, u32[]{:S(2)}) copy-start(bf16[512,1024]{1,0:T(8,128)(2,1)} %copy-done.3) | copy-start | bytes 3145732
  36.9 6.4 %copy-start.7 = (bf16[4,128,512]{2,1,0:T(8,128)(2,1)S(1)}, bf16[4,128,512]{2,1,0:T(8,128)(2,1)}, u32[]{:S(2)}) copy-start(bf16[4,128,512]{2,1,0:T(8,128)(2,1)} %copy-done.6) | copy-start | bytes 1572868
  38.4 7.5 %collective-permute-start.1 = (bf16[64,1152]{1,0:T(8,128)(2,1)S(1)}, bf16[64,1152]{1,0:T(8,128)(2,1)S(1)}, u32[]{:S(2)}, u32[]{:S(2)}) collective-permute-start(bf16[64,1152]{1,0:T(8,128)(2,1)S(1)} %get-tuple-element.33), channel_id=1, source_target_pairs={{1,0},{2,1},{3,2},{4,3},{5,4},{6,5},{7,6},{0,7},{9,8},{10,9},{11,1... | collective-permute-start | bytes 442376 | tf_op jit(solution)/shard_map/ppermute | solution.py:235
  42.3 11.1 %collective-permute-start = (bf16[64,1152]{1,0:T(8,128)(2,1)S(1)}, bf16[64,1152]{1,0:T(8,128)(2,1)S(1)}, u32[]{:S(2)}, u32[]{:S(2)}) collective-permute-start(bf16[64,1152]{1,0:T(8,128)(2,1)S(1)} %get-tuple-element.32.token_ref), channel_id=1, source_target_pairs={{0,1},{1,2},{2,3},{3,4},{4,5},{5,6},{6,7},{7,0},{8,9},{9,10},{10,1... | collective-permute-start | bytes 442376 | tf_op jit(solution)/shard_map/ppermute | solution.py:234
  42.4 12.4 %collective-permute-start.6 = (bf16[160,640]{1,0:T(8,128)(2,1)S(1)}, bf16[160,640]{1,0:T(8,128)(2,1)S(1)}, u32[]{:S(2)}, u32[]{:S(2)}) collective-permute-start(bf16[160,640]{1,0:T(8,128)(2,1)S(1)} %get-tuple-element.45), channel_id=1, source_target_pairs={{0,8},{8,16},{16,24},{24,32},{32,40},{40,48},{48,56},{56,64},{64,7... | collective-permute-start | bytes 614408 | tf_op jit(solution)/shard_map/ppermute | solution.py:234
  43.3 11.5 %collective-permute-start.7 = (bf16[160,640]{1,0:T(8,128)(2,1)S(1)}, bf16[160,640]{1,0:T(8,128)(2,1)S(1)}, u32[]{:S(2)}, u32[]{:S(2)}) collective-permute-start(bf16[160,640]{1,0:T(8,128)(2,1)S(1)} %get-tuple-element.40.token_ref), channel_id=1, source_target_pairs={{8,0},{16,8},{24,16},{32,24},{40,32},{48,40},{56,48},{64,56},{72,6... | collective-permute-start | bytes 614408 | tf_op jit(solution)/shard_map/ppermute | solution.py:235
  43.3 11.5 %copy-start.9 = (f32[4,128,128]{2,1,0:T(8,128)S(1)}, f32[4,128,128]{2,1,0:T(8,128)}, u32[]{:S(2)}) copy-start(f32[4,128,128]{2,1,0:T(8,128)} %copy-done.8) | copy-start | bytes 786436
  53.5 10.6 %collective-permute-start.4 = (bf16[160,1152]{1,0:T(8,128)(2,1)S(1)}, bf16[160,1152]{1,0:T(8,128)(2,1)S(1)}, u32[]{:S(2)}, u32[]{:S(2)}) collective-permute-start(bf16[160,1152]{1,0:T(8,128)(2,1)S(1)} %get-tuple-element.41), channel_id=1, source_target_pairs={{0,8},{8,16},{16,24},{24,32},{32,40},{40,48},{48,56},{56,64},{64,7... | collective-permute-start | bytes 1105928 | tf_op jit(solution)/shard_map/ppermute | solution.py:234
  53.6 10.5 %collective-permute-start.5 = (bf16[160,1152]{1,0:T(8,128)(2,1)S(1)}, bf16[160,1152]{1,0:T(8,128)(2,1)S(1)}, u32[]{:S(2)}, u32[]{:S(2)}) collective-permute-start(bf16[160,1152]{1,0:T(8,128)(2,1)S(1)} %get-tuple-element.42.token_ref), channel_id=1, source_target_pairs={{8,0},{16,8},{24,16},{32,24},{40,32},{48,40},{56,48},{64,56},{72,6... | collective-permute-start | bytes 1105928 | tf_op jit(solution)/shard_map/ppermute | solution.py:235
  68.7 25.2 %all-to-all-start.1 = ((bf16[128,8,512]{2,1,0:T(8,128)(2,1)}), bf16[128,8,512]{2,1,0:T(8,128)(2,1)S(1)}, u32[]{:S(2)}, u32[]{:S(2)}) async-start(bf16[128,8,512]{2,1,0:T(8,128)(2,1)} %bitcast.16), calls=%async_computation.1 | async-start | bytes 2097152 | tf_op jit(solution)/shard_map/all_to_all | solution.py:562
  75.7 18.1 %copy-start.5 = (s32[512,128]{1,0:T(8,128)S(1)}, s32[512,128]{1,0:T(8,128)}, u32[]{:S(2)}) copy-start(s32[512,128]{1,0:T(8,128)} %get-tuple-element.53.place_ref) | copy-start | bytes 786436

commit v3 on v2

--- a/solution.py
+++ b/solution.py
@@ -26,7 +26,6 @@
 WIDE = H * (CY + 2 * H)
 HALO = 2 * SIDE + 2 * WIDE
 PANEL = 16
-SPLIT = 64
 
 BF = jnp.bfloat16
 F32 = jnp.float32
@@ -113,7 +112,6 @@
     cs = _iota((ROWS, ROWS), 1)
     within = jnp.sum(jnp.where(same & (rs < cs), 1.0, 0.0), axis=0, keepdims=True)
     place = jnp.where(valid, ownf * CAP + within, -64.0).astype(jnp.int32)
-    place_ref[...] = jnp.broadcast_to(place.astype(F32), (LANE, ROWS)).T.astype(jnp.int32)
     meta_b = meta_t.astype(BF)
     load.wait()
     step = 128
@@ -129,6 +127,7 @@
         store = pltpu.make_async_copy(send_ref.at[out], send_hbm.at[out], out_sem.at[i])
         store.start()
         stores.append(store)
+    place_ref[...] = jnp.broadcast_to(place.astype(F32), (LANE, ROWS)).T.astype(jnp.int32)
     for store in stores:
         store.wait()
 
@@ -383,25 +382,25 @@
     )(core)
 
 
-def _inverse_first_body(gram_ref, before_ref, after_ref, up_ref, down_ref, v_ref, token_ref, lth_ref, seen_ref, pred_ref, part_ref):
+def _inverse_body(gram_ref, before_ref, after_ref, up_ref, down_ref, v_ref, token_ref, lth_ref, seen_ref, pred_ref, inv_ref):
     halos = (before_ref, after_ref, up_ref, down_ref)
     for f in range(FOLDS):
         halo = jnp.concatenate([r[:, f * RANK : (f + 1) * RANK] for r in halos], axis=0)
         halo_t = halo.T
         lth_ref[f] = halo_t
-        part_ref[f] = gram_ref[f] + _dot(halo_t, halo)
+        inv_ref[f] = gram_ref[f] + _dot(halo_t, halo)
         pred_ref[f] = _dot_nt(halo, v_ref[f]).astype(BF)
     at = 0
     for ref in halos:
         n = ref.shape[0]
         seen_ref[at : at + n, :] = _unpack(ref[:, FOLDS * RANK :])
         at += n
-    _eliminate(part_ref, 0, SPLIT)
-
-
-def _inverse_first(gram, before, after, up, down, v, token):
-    return pl.pallas_call(
-        _inverse_first_body,
+    _eliminate(inv_ref, 0, RANK)
+
+
+def _inverse(gram, before, after, up, down, v, token):
+    return pl.pallas_call(
+        _inverse_body,
         in_specs=[_VMEM] * 6 + [_ANY],
         out_shape=(
             jax.ShapeDtypeStruct((FOLDS, RANK, HALO), BF),
@@ -411,24 +410,8 @@
         ),
         compiler_params=_params(),
         cost_estimate=_cost(4 * 10**9, 4 * 10**6),
-        name="inverse_first",
+        name="gram_inverse",
     )(gram, before, after, up, down, v, token)
-
-
-def _inverse_second_body(part_ref, token_ref, inv_ref):
-    inv_ref[...] = part_ref[...]
-    _eliminate(inv_ref, SPLIT, RANK)
-
-
-def _inverse_second(part, token):
-    return pl.pallas_call(
-        _inverse_second_body,
-        in_specs=[_VMEM, _ANY],
-        out_shape=jax.ShapeDtypeStruct((FOLDS, RANK, RANK), F32),
-        compiler_params=_params(),
-        cost_estimate=_cost(4 * 10**9, 10**6),
-        name="inverse_second",
-    )(part, token)
 
 
 def _threshold(foldp, f):
@@ -574,10 +557,9 @@
     lpack = _pack(lbefore, lafter, ltop, lbot, right, True, "margin_left")
     lhalos = (lbefore, lafter, *_along(*lpack, "mlong"))
     cross = _core_cross(data, seen_c, lext, ltc, right_factors)
-    lth, seen_h, pred_h, part = _inverse_first(gram, *lhalos, right_factors, top)
     pack = _pack(before, after, top, bot, lpack[0], False, "margin_data")
     halos = (before, after, *_along(*pack, "mlong"))
-    inv = _inverse_second(part, pack[0])
+    lth, seen_h, pred_h, inv = _inverse(gram, *lhalos, right_factors, pack[0])
     back, new = _final(data, halos, seen_c, seen_h, lext, lth, pred_h, cross, inv, got)
     ret = _swap(back)
     new_right = _turn(new)

time: 96 us -> 95.8 us (level)
    pallas_call x2 -> x1, Pallas kernels: 9.22 us -> 9.19 us  [_inverse(): pl.pallas_call(_inverse_body, in_specs=[_VMEM] * 6 + [_ANY], out_shape=(j...]
where the time goes in v3:
time: 95.8 us; the launch traced here: 95.6 us
  waiting for transfers between devices  35.6 us (37%)
  starting transfers between devices  30.1 us (31%)
  Pallas kernels  26.1 us (27%)
  local copies, waits for them, and re-layouts  2.72 us (3%)
  between operations  1.02 us (1%)
    all_to_all x2, waiting for transfers between devices, _swap(): return lax.all_to_all(x, AXES, split_axis=0, concat_axis=0, tiled=True)  27.4 us
    all_to_all x2, starting transfers between devices, _swap(): return lax.all_to_all(x, AXES, split_axis=0, concat_axis=0, tiled=True)  18.5 us
    ppermute x4, starting transfers between devices, _along(): after = lax.ppermute(to_up, axis, [(j, i) for i, j in fwd])  9.24 us
    pallas_call x1, Pallas kernels, _inverse(): pl.pallas_call(_inverse_body, in_specs=[_VMEM] * 6 + [_ANY], out_shape=(j...  9.19 us
    ppermute x4, waiting for transfers between devices, _along(): before = lax.ppermute(to_down, axis, fwd)  7.44 us
    pallas_call x1, Pallas kernels, _final(): pl.pallas_call(_final_body, in_specs=[_VMEM] * 13, out_specs=(_HBM, _VMEM...  4.5 us
    pallas_call x1, Pallas kernels, _route(): pl.pallas_call(_route_body, in_specs=[_HBM] * 4, out_specs=(_HBM, _VMEM),...  3.7 us
    unnamed x26, local copies, waits for them, and re-layouts  2.72 us
  transfers between devices with their start and end apart: 10, of which 4 were waited for; matrix products, arithmetic and copies ran while one was open for 0% of the time, Pallas kernels for 17%

profile of v3, /device:TPU:1, one launch (start us, length us, event | category | flops | bytes accessed | tf_op | source)
XLA Modules:
  0.0 95.6 jit_solution(10494150173826855768)
XLA Ops:
  0.6 3.7 %route.1 = (bf16[1024,640]{1,0:T(8,128)(2,1)}, s32[512,128]{1,0:T(8,128)}) custom-call(s32[1,512]{1,0:T(1,128)} %bitcast.18, s32[1,512]{1,0:T(1,128)} %bitcast.19, s32[1,512]{1,0:T(1,128)} %bitcast.20, bf16[512,1024]{1,0:T(8,128)(2,1)} %tr_hbm.1), custom_call_target="tpu_custom_call" | custom-call | flops 1000000000 | bytes 4000000 | tf_op jit(solution)/shard_map/route/pallas_call | solution.py:136
  4.3 0.0 copy-start.11
  4.3 0.0 copy-start.10
  4.4 11.5 %all-to-all-start = ((bf16[128,8,640]{2,1,0:T(8,128)(2,1)}), bf16[128,8,640]{2,1,0:T(8,128)(2,1)S(1)}, u32[]{:S(2)}, u32[]{:S(2)}) async-start(bf16[128,8,640]{2,1,0:T(8,128)(2,1)} %bitcast.15), calls=%async_computation | async-start | bytes 2621440 | tf_op jit(solution)/shard_map/all_to_all | solution.py:545
  15.9 0.1 copy.9.bits_ref
  16.0 0.1 copy.12
  16.1 0.4 left_rows.1
  16.6 1.5 %collective-permute-start.2 = (bf16[64,640]{1,0:T(8,128)(2,1)S(1)}, bf16[64,640]{1,0:T(8,128)(2,1)S(1)}, u32[]{:S(2)}, u32[]{:S(2)}) collective-permute-start(bf16[64,640]{1,0:T(8,128)(2,1)S(1)} %get-tuple-element.36), channel_id=1, source_target_pairs={{0,1},{1,2},{2,3},{3,4},{4,5},{5,6},{6,7},{7,0},{8,9},{9,10},{10,1... | collective-permute-start | bytes 245768 | tf_op jit(solution)/shard_map/ppermute | solution.py:233
  18.0 4.1 %collective-permute-start.3 = (bf16[64,640]{1,0:T(8,128)(2,1)S(1)}, bf16[64,640]{1,0:T(8,128)(2,1)S(1)}, u32[]{:S(2)}, u32[]{:S(2)}) collective-permute-start(bf16[64,640]{1,0:T(8,128)(2,1)S(1)} %get-tuple-element.37), channel_id=1, source_target_pairs={{1,0},{2,1},{3,2},{4,3},{5,4},{6,5},{7,6},{0,7},{9,8},{10,9},{11,1... | collective-permute-start | bytes 245768 | tf_op jit(solution)/shard_map/ppermute | solution.py:234
  22.2 0.7 core_prep.1
  22.9 0.0 copy-start.3
  22.9 1.0 %copy-done.3 = bf16[512,1024]{1,0:T(8,128)(2,1)} copy-done((bf16[512,1024]{1,0:T(8,128)(2,1)}, bf16[512,1024]{1,0:T(8,128)(2,1)S(1)}, u32[]{:S(2)}) %copy-start.3) | copy-done | bytes 1048600
  23.9 0.8 copy-done.6
  24.7 0.7 copy-done.8
  25.4 11.5 %all-to-all-done = bf16[128,8,640]{2,1,0:T(8,128)(2,1)S(1)} async-done(((bf16[128,8,640]{2,1,0:T(8,128)(2,1)}), bf16[128,8,640]{2,1,0:T(8,128)(2,1)S(1)}, u32[]{:S(2)}, u32[]{:S(2)}) %all-to-all-start) | async-done | bytes 1310752 | tf_op jit(solution)/shard_map/all_to_all | solution.py:545
  36.9 1.5 %to_grid.1 = (bf16[512,1152]{1,0:T(8,128)(2,1)S(1)}, bf16[128,1152]{1,0:T(8,128)(2,1)S(1)}, bf16[128,1152]{1,0:T(8,128)(2,1)S(1)}, bf16[64,1152]{1,0:T(8,128)(2,1)S(1)}, bf16[64,1152]{1,0:T(8,128)(2,1)S(1)}) custom-call(bf16[1024,640]{1,0:T(8,128)(2,1)S(1)} %bitcast.12, f32[8,128]{1,0:T(8,128)S(1)} %get-tuple-element.30.after_ref), custom_call_target="tpu_custom_call" | custom-call | flops 1000000000 | bytes 4000000 | tf_op jit(solution)/shard_map/to_grid/pallas_call | solution.py:189
  38.4 3.9 %collective-permute-start.1 = (bf16[64,1152]{1,0:T(8,128)(2,1)S(1)}, bf16[64,1152]{1,0:T(8,128)(2,1)S(1)}, u32[]{:S(2)}, u32[]{:S(2)}) collective-permute-start(bf16[64,1152]{1,0:T(8,128)(2,1)S(1)} %get-tuple-element.33), channel_id=1, source_target_pairs={{1,0},{2,1},{3,2},{4,3},{5,4},{6,5},{7,6},{0,7},{9,8},{10,9},{11,1... | collective-permute-start | bytes 442376 | tf_op jit(solution)/shard_map/ppermute | solution.py:234
  42.3 0.0 collective-permute-start
  42.3 0.1 margin_left.1
  42.4 0.8 collective-permute-start.6
  43.3 1.9 %cross_core.1.cross_ref = f32[4,128,1024]{2,1,0:T(8,128)S(1)} custom-call(bf16[512,1152]{1,0:T(8,128)(2,1)S(1)} %get-tuple-element.31.data_ref, bf16[512,1024]{1,0:T(8,128)(2,1)S(1)} %copy-done.4, bf16[512,640]{1,0:T(8,128)(2,1)S(1)} %copy-done.2, bf16[4,128,512]{2,1,0:T(8,128)(2,1)S(1)} %copy-done.7, bf16[4,1024,128]{2,1,0:T(8,128)(2,1)S(1)} %copy-done), custom_call_target="tpu_custom_call" | custom-call | flops 3000000000 | bytes 6000000 | tf_op jit(solution)/shard_map/cross_core/pallas_call | solution.py:436
  45.2 0.8 collective-permute-done.1.after_ref
  46.0 7.4 %collective-permute-done.before_ref = bf16[64,1152]{1,0:T(8,128)(2,1)S(1)} collective-permute-done((bf16[64,1152]{1,0:T(8,128)(2,1)S(1)}, bf16[64,1152]{1,0:T(8,128)(2,1)S(1)}, u32[]{:S(2)}, u32[]{:S(2)}) %collective-permute-start) | collective-permute-done | bytes 147488 | tf_op jit(solution)/shard_map/ppermute | solution.py:233
  53.4 0.1 margin_data.1
  53.5 0.1 collective-permute-start.4
  53.6 1.2 %collective-permute-start.5 = (bf16[160,1152]{1,0:T(8,128)(2,1)S(1)}, bf16[160,1152]{1,0:T(8,128)(2,1)S(1)}, u32[]{:S(2)}, u32[]{:S(2)}) collective-permute-start(bf16[160,1152]{1,0:T(8,128)(2,1)S(1)} %get-tuple-element.42.token_ref), channel_id=1, source_target_pairs={{8,0},{16,8},{24,16},{32,24},{40,32},{48,40},{56,48},{64,56},{72,6... | collective-permute-start | bytes 1105928 | tf_op jit(solution)/shard_map/ppermute | solution.py:234
  54.8 9.2 %gram_inverse.1 = (bf16[4,128,448]{2,1,0:T(8,128)(2,1)S(1)}, bf16[448,1024]{1,0:T(8,128)(2,1)S(1)}, bf16[4,448,1024]{2,1,0:T(8,128)(2,1)S(1)}, f32[4,128,128]{2,1,0:T(8,128)S(1)}) custom-call(f32[4,128,128]{2,1,0:T(8,128)S(1)} %copy-done.9, bf16[64,640]{1,0:T(8,128)(2,1)S(1)} %collective-permute-done.2.before_ref, ...), custom_call_target="tpu_custom_call" | custom-call | flops 4000000000 | bytes 4000000 | tf_op jit(solution)/shard_map/gram_inverse/pallas_call | solution.py:402
  64.0 4.5 %update_residual.1 = (bf16[1024,512]{1,0:T(8,128)(2,1)}, f32[4,128,1024]{2,1,0:T(8,128)S(1)}) custom-call(bf16[512,1152]{1,0:T(8,128)(2,1)S(1)} %get-tuple-element.31.data_ref, bf16[64,1152]{1,0:T(8,128)(2,1)S(1)} %collective-permute-done.before_ref, bf16[64,1152]{1,0:T(8,128)(2,1)S(1)} %collective-permute-done.1.after_ref, ...), custom_call_target="tpu_custom_call" | custom-call | flops 4000000000 | bytes 10000000 | tf_op jit(solution)/shard_map/update_residual/pallas_call | solution.py:485
  68.5 7.0 %all-to-all-start.1 = ((bf16[128,8,512]{2,1,0:T(8,128)(2,1)}), bf16[128,8,512]{2,1,0:T(8,128)(2,1)S(1)}, u32[]{:S(2)}, u32[]{:S(2)}) async-start(bf16[128,8,512]{2,1,0:T(8,128)(2,1)} %bitcast.16), calls=%async_computation.1 | async-start | bytes 2097152 | tf_op jit(solution)/shard_map/all_to_all | solution.py:545
  75.6 2.2 %new_right.1 = f32[4,1024,128]{2,1,0:T(8,128)} custom-call(f32[4,128,1024]{2,1,0:T(8,128)S(1)} %get-tuple-element.51.new_ref), custom_call_target="tpu_custom_call" | custom-call | flops 1000000 | bytes 4000000 | tf_op jit(solution)/shard_map/new_right/pallas_call | solution.py:505
  77.8 15.9 %all-to-all-done.1 = bf16[128,8,512]{2,1,0:T(8,128)(2,1)S(1)} async-done(((bf16[128,8,512]{2,1,0:T(8,128)(2,1)}), bf16[128,8,512]{2,1,0:T(8,128)(2,1)S(1)}, u32[]{:S(2)}, u32[]{:S(2)}) %all-to-all-start.1) | async-done | bytes 1048608 | tf_op jit(solution)/shard_map/all_to_all | solution.py:545
  93.7 1.7 %give_back.1 = bf16[512,1024]{1,0:T(8,128)(2,1)} custom-call(bf16[1024,512]{1,0:T(8,128)(2,1)S(1)} %bitcast.14, s32[512,128]{1,0:T(8,128)S(1)} %copy-done.5), custom_call_target="tpu_custom_call" | custom-call | flops 1000000000 | bytes 4000000 | tf_op jit(solution)/shard_map/give_back/pallas_call | solution.py:532
  (25 shorter events, 0.1 us)
Async XLA Ops:
  4.3 11.5 %copy-start.11 = (s32[512,64]{0,1:T(8,128)S(1)}, s32[512,64]{0,1:T(8,128)}, u32[]{:S(2)}) copy-start(s32[512,64]{0,1:T(8,128)} %param.11) | copy-start | bytes 393220
  4.3 11.7 %copy-start.10 = (bf16[512,4,128]{2,1,0:T(4,128)(2,1)S(1)}, bf16[512,4,128]{2,1,0:T(4,128)(2,1)}, u32[]{:S(2)}) copy-start(bf16[512,4,128]{2,1,0:T(4,128)(2,1)} %param.12) | copy-start | bytes 1572868
  4.4 32.5 %all-to-all-start = ((bf16[128,8,640]{2,1,0:T(8,128)(2,1)}), bf16[128,8,640]{2,1,0:T(8,128)(2,1)S(1)}, u32[]{:S(2)}, u32[]{:S(2)}) async-start(bf16[128,8,640]{2,1,0:T(8,128)(2,1)} %bitcast.15), calls=%async_computation | async-start | bytes 2621440 | tf_op jit(solution)/shard_map/all_to_all | solution.py:545
  16.6 20.3 %copy-start.1 = (bf16[512,640]{1,0:T(8,128)(2,1)}, bf16[512,640]{1,0:T(8,128)(2,1)S(1)}, u32[]{:S(2)}) copy-start(bf16[512,640]{1,0:T(8,128)(2,1)S(1)} %get-tuple-element.29.core_ref.l_ref.lc_ref) | copy-start | bytes 1966084
  16.6 25.8 %collective-permute-start.2 = (bf16[64,640]{1,0:T(8,128)(2,1)S(1)}, bf16[64,640]{1,0:T(8,128)(2,1)S(1)}, u32[]{:S(2)}, u32[]{:S(2)}) collective-permute-start(bf16[64,640]{1,0:T(8,128)(2,1)S(1)} %get-tuple-element.36), channel_id=1, source_target_pairs={{0,1},{1,2},{2,3},{3,4},{4,5},{5,6},{6,7},{7,0},{8,9},{9,10},{10,1... | collective-permute-start | bytes 245768 | tf_op jit(solution)/shard_map/ppermute | solution.py:233
  18.0 24.3 %collective-permute-start.3 = (bf16[64,640]{1,0:T(8,128)(2,1)S(1)}, bf16[64,640]{1,0:T(8,128)(2,1)S(1)}, u32[]{:S(2)}, u32[]{:S(2)}) collective-permute-start(bf16[64,640]{1,0:T(8,128)(2,1)S(1)} %get-tuple-element.37), channel_id=1, source_target_pairs={{1,0},{2,1},{3,2},{4,3},{5,4},{6,5},{7,6},{0,7},{9,8},{10,9},{11,1... | collective-permute-start | bytes 245768 | tf_op jit(solution)/shard_map/ppermute | solution.py:234
  22.9 1.0 %copy-start.3 = (bf16[512,1024]{1,0:T(8,128)(2,1)}, bf16[512,1024]{1,0:T(8,128)(2,1)S(1)}, u32[]{:S(2)}) copy-start(bf16[512,1024]{1,0:T(8,128)(2,1)S(1)} %get-tuple-element.43.seen_ref.seen_c_ref) | copy-start | bytes 3145732
  23.9 0.8 copy-start.6
  24.7 0.7 copy-start.8
  36.9 6.4 %copy-start = (bf16[4,1024,128]{2,1,0:T(8,128)(2,1)S(1)}, bf16[4,1024,128]{2,1,0:T(8,128)(2,1)}, u32[]{:S(2)}) copy-start(bf16[4,1024,128]{2,1,0:T(8,128)(2,1)} %v_ref.3) | copy-start | bytes 3145732
  36.9 6.4 %copy-start.2 = (bf16[512,640]{1,0:T(8,128)(2,1)S(1)}, bf16[512,640]{1,0:T(8,128)(2,1)}, u32[]{:S(2)}) copy-start(bf16[512,640]{1,0:T(8,128)(2,1)} %copy-done.1) | copy-start | bytes 1966084
  36.9 6.4 %copy-start.4 = (bf16[512,1024]{1,0:T(8,128)(2,1)S(1)}, bf16[512,1024]{1,0:T(8,128)(2,1)}, u32[]{:S(2)}) copy-start(bf16[512,1024]{1,0:T(8,128)(2,1)} %copy-done.3) | copy-start | bytes 3145732
  36.9 6.4 %copy-start.7 = (bf16[4,128,512]{2,1,0:T(8,128)(2,1)S(1)}, bf16[4,128,512]{2,1,0:T(8,128)(2,1)}, u32[]{:S(2)}) copy-start(bf16[4,128,512]{2,1,0:T(8,128)(2,1)} %copy-done.6) | copy-start | bytes 1572868
  38.4 7.5 %collective-permute-start.1 = (bf16[64,1152]{1,0:T(8,128)(2,1)S(1)}, bf16[64,1152]{1,0:T(8,128)(2,1)S(1)}, u32[]{:S(2)}, u32[]{:S(2)}) collective-permute-start(bf16[64,1152]{1,0:T(8,128)(2,1)S(1)} %get-tuple-element.33), channel_id=1, source_target_pairs={{1,0},{2,1},{3,2},{4,3},{5,4},{6,5},{7,6},{0,7},{9,8},{10,9},{11,1... | collective-permute-start | bytes 442376 | tf_op jit(solution)/shard_map/ppermute | solution.py:234
  42.3 11.1 %collective-permute-start = (bf16[64,1152]{1,0:T(8,128)(2,1)S(1)}, bf16[64,1152]{1,0:T(8,128)(2,1)S(1)}, u32[]{:S(2)}, u32[]{:S(2)}) collective-permute-start(bf16[64,1152]{1,0:T(8,128)(2,1)S(1)} %get-tuple-element.32.token_ref), channel_id=1, source_target_pairs={{0,1},{1,2},{2,3},{3,4},{4,5},{5,6},{6,7},{7,0},{8,9},{9,10},{10,1... | collective-permute-start | bytes 442376 | tf_op jit(solution)/shard_map/ppermute | solution.py:233
  42.4 12.4 %collective-permute-start.6 = (bf16[160,640]{1,0:T(8,128)(2,1)S(1)}, bf16[160,640]{1,0:T(8,128)(2,1)S(1)}, u32[]{:S(2)}, u32[]{:S(2)}) collective-permute-start(bf16[160,640]{1,0:T(8,128)(2,1)S(1)} %get-tuple-element.45), channel_id=1, source_target_pairs={{0,8},{8,16},{16,24},{24,32},{32,40},{40,48},{48,56},{56,64},{64,7... | collective-permute-start | bytes 614408 | tf_op jit(solution)/shard_map/ppermute | solution.py:233
  43.3 11.5 %collective-permute-start.7 = (bf16[160,640]{1,0:T(8,128)(2,1)S(1)}, bf16[160,640]{1,0:T(8,128)(2,1)S(1)}, u32[]{:S(2)}, u32[]{:S(2)}) collective-permute-start(bf16[160,640]{1,0:T(8,128)(2,1)S(1)} %get-tuple-element.40.token_ref), channel_id=1, source_target_pairs={{8,0},{16,8},{24,16},{32,24},{40,32},{48,40},{56,48},{64,56},{72,6... | collective-permute-start | bytes 614408 | tf_op jit(solution)/shard_map/ppermute | solution.py:234
  43.3 11.5 %copy-start.9 = (f32[4,128,128]{2,1,0:T(8,128)S(1)}, f32[4,128,128]{2,1,0:T(8,128)}, u32[]{:S(2)}) copy-start(f32[4,128,128]{2,1,0:T(8,128)} %copy-done.8) | copy-start | bytes 786436
  53.5 10.5 %collective-permute-start.4 = (bf16[160,1152]{1,0:T(8,128)(2,1)S(1)}, bf16[160,1152]{1,0:T(8,128)(2,1)S(1)}, u32[]{:S(2)}, u32[]{:S(2)}) collective-permute-start(bf16[160,1152]{1,0:T(8,128)(2,1)S(1)} %get-tuple-element.41), channel_id=1, source_target_pairs={{0,8},{8,16},{16,24},{24,32},{32,40},{40,48},{48,56},{56,64},{64,7... | collective-permute-start | bytes 1105928 | tf_op jit(solution)/shard_map/ppermute | solution.py:233
  53.6 10.4 %collective-permute-start.5 = (bf16[160,1152]{1,0:T(8,128)(2,1)S(1)}, bf16[160,1152]{1,0:T(8,128)(2,1)S(1)}, u32[]{:S(2)}, u32[]{:S(2)}) collective-permute-start(bf16[160,1152]{1,0:T(8,128)(2,1)S(1)} %get-tuple-element.42.token_ref), channel_id=1, source_target_pairs={{8,0},{16,8},{24,16},{32,24},{40,32},{48,40},{56,48},{64,56},{72,6... | collective-permute-start | bytes 1105928 | tf_op jit(solution)/shard_map/ppermute | solution.py:234
  68.5 25.2 %all-to-all-start.1 = ((bf16[128,8,512]{2,1,0:T(8,128)(2,1)}), bf16[128,8,512]{2,1,0:T(8,128)(2,1)S(1)}, u32[]{:S(2)}, u32[]{:S(2)}) async-start(bf16[128,8,512]{2,1,0:T(8,128)(2,1)} %bitcast.16), calls=%async_computation.1 | async-start | bytes 2097152 | tf_op jit(solution)/shard_map/all_to_all | solution.py:545
  75.5 18.1 %copy-start.5 = (s32[512,128]{1,0:T(8,128)S(1)}, s32[512,128]{1,0:T(8,128)}, u32[]{:S(2)}) copy-start(s32[512,128]{1,0:T(8,128)} %get-tuple-element.53.place_ref) | copy-start | bytes 786436

commit v4 on v2

--- a/solution.py
+++ b/solution.py
@@ -49,7 +49,7 @@
     return lax.dot_general(a, b, (((1,), (1,)), ((), ())), preferred_element_type=F32)
 
 
-def _params(limit=32):
+def _params(limit=20):
     return pltpu.CompilerParams(vmem_limit_bytes=limit * 1024 * 1024)
 
 

time: 96 us -> 96 us (level)
  no operation moved by 1% of the time
where the time goes in v4:
time: 96 us; the launch traced here: 95.7 us
  waiting for transfers between devices  35.6 us (37%)
  starting transfers between devices  30.2 us (31%)
  Pallas kernels  26.2 us (27%)
  local copies, waits for them, and re-layouts  2.72 us (3%)
  between operations  1.02 us (1%)
    all_to_all x2, waiting for transfers between devices, _swap(): return lax.all_to_all(x, AXES, split_axis=0, concat_axis=0, tiled=True)  27.4 us
    all_to_all x2, starting transfers between devices, _swap(): return lax.all_to_all(x, AXES, split_axis=0, concat_axis=0, tiled=True)  18.6 us
    ppermute x4, starting transfers between devices, _along(): after = lax.ppermute(to_up, axis, [(j, i) for i, j in fwd])  9.25 us
    ppermute x4, waiting for transfers between devices, _along(): before = lax.ppermute(to_down, axis, fwd)  7.44 us
    pallas_call x1, Pallas kernels, _inverse_first(): pl.pallas_call(_inverse_first_body, in_specs=[_VMEM] * 6 + [_ANY], out_sh...  5.26 us
    pallas_call x1, Pallas kernels, _final(): pl.pallas_call(_final_body, in_specs=[_VMEM] * 13, out_specs=(_HBM, _VMEM...  4.6 us
    pallas_call x1, Pallas kernels, _inverse_second(): pl.pallas_call(_inverse_second_body, in_specs=[_VMEM, _ANY], out_shape=ja...  3.96 us
    pallas_call x1, Pallas kernels, _route(): pl.pallas_call(_route_body, in_specs=[_HBM] * 4, out_specs=(_HBM, _VMEM),...  3.7 us
  transfers between devices with their start and end apart: 10, of which 4 were waited for; matrix products, arithmetic and copies ran while one was open for 0% of the time, Pallas kernels for 17%

profile of v4, /device:TPU:1, one launch (start us, length us, event | category | flops | bytes accessed | tf_op | source)
XLA Modules:
  0.0 95.7 jit_solution(7714257620324377646)
XLA Ops:
  0.6 3.7 %route.1 = (bf16[1024,640]{1,0:T(8,128)(2,1)}, s32[512,128]{1,0:T(8,128)}) custom-call(s32[1,512]{1,0:T(1,128)} %bitcast.18, s32[1,512]{1,0:T(1,128)} %bitcast.19, s32[1,512]{1,0:T(1,128)} %bitcast.20, bf16[512,1024]{1,0:T(8,128)(2,1)} %tr_hbm.1), custom_call_target="tpu_custom_call" | custom-call | flops 1000000000 | bytes 4000000 | tf_op jit(solution)/shard_map/route/pallas_call | solution.py:137
  4.3 0.0 copy-start.11
  4.3 0.0 copy-start.10
  4.4 11.5 %all-to-all-start = ((bf16[128,8,640]{2,1,0:T(8,128)(2,1)}), bf16[128,8,640]{2,1,0:T(8,128)(2,1)S(1)}, u32[]{:S(2)}, u32[]{:S(2)}) async-start(bf16[128,8,640]{2,1,0:T(8,128)(2,1)} %bitcast.15), calls=%async_computation | async-start | bytes 2621440 | tf_op jit(solution)/shard_map/all_to_all | solution.py:562
  15.9 0.1 copy.9.bits_ref
  16.0 0.1 copy.12
  16.1 0.4 left_rows.1
  16.6 1.5 %collective-permute-start.2 = (bf16[64,640]{1,0:T(8,128)(2,1)S(1)}, bf16[64,640]{1,0:T(8,128)(2,1)S(1)}, u32[]{:S(2)}, u32[]{:S(2)}) collective-permute-start(bf16[64,640]{1,0:T(8,128)(2,1)S(1)} %get-tuple-element.36), channel_id=1, source_target_pairs={{0,1},{1,2},{2,3},{3,4},{4,5},{5,6},{6,7},{7,0},{8,9},{9,10},{10,1... | collective-permute-start | bytes 245768 | tf_op jit(solution)/shard_map/ppermute | solution.py:234
  18.0 4.1 %collective-permute-start.3 = (bf16[64,640]{1,0:T(8,128)(2,1)S(1)}, bf16[64,640]{1,0:T(8,128)(2,1)S(1)}, u32[]{:S(2)}, u32[]{:S(2)}) collective-permute-start(bf16[64,640]{1,0:T(8,128)(2,1)S(1)} %get-tuple-element.37), channel_id=1, source_target_pairs={{1,0},{2,1},{3,2},{4,3},{5,4},{6,5},{7,6},{0,7},{9,8},{10,9},{11,1... | collective-permute-start | bytes 245768 | tf_op jit(solution)/shard_map/ppermute | solution.py:235
  22.2 0.7 core_prep.1
  22.9 0.0 copy-start.3
  22.9 1.0 %copy-done.3 = bf16[512,1024]{1,0:T(8,128)(2,1)} copy-done((bf16[512,1024]{1,0:T(8,128)(2,1)}, bf16[512,1024]{1,0:T(8,128)(2,1)S(1)}, u32[]{:S(2)}) %copy-start.3) | copy-done | bytes 1048600
  23.9 0.8 copy-done.6
  24.7 0.7 copy-done.8
  25.4 11.5 %all-to-all-done = bf16[128,8,640]{2,1,0:T(8,128)(2,1)S(1)} async-done(((bf16[128,8,640]{2,1,0:T(8,128)(2,1)}), bf16[128,8,640]{2,1,0:T(8,128)(2,1)S(1)}, u32[]{:S(2)}, u32[]{:S(2)}) %all-to-all-start) | async-done | bytes 1310752 | tf_op jit(solution)/shard_map/all_to_all | solution.py:562
  36.9 1.5 %to_grid.1 = (bf16[512,1152]{1,0:T(8,128)(2,1)S(1)}, bf16[128,1152]{1,0:T(8,128)(2,1)S(1)}, bf16[128,1152]{1,0:T(8,128)(2,1)S(1)}, bf16[64,1152]{1,0:T(8,128)(2,1)S(1)}, bf16[64,1152]{1,0:T(8,128)(2,1)S(1)}) custom-call(bf16[1024,640]{1,0:T(8,128)(2,1)S(1)} %bitcast.12, f32[8,128]{1,0:T(8,128)S(1)} %get-tuple-element.30.after_ref), custom_call_target="tpu_custom_call" | custom-call | flops 1000000000 | bytes 4000000 | tf_op jit(solution)/shard_map/to_grid/pallas_call | solution.py:190
  38.4 3.9 %collective-permute-start.1 = (bf16[64,1152]{1,0:T(8,128)(2,1)S(1)}, bf16[64,1152]{1,0:T(8,128)(2,1)S(1)}, u32[]{:S(2)}, u32[]{:S(2)}) collective-permute-start(bf16[64,1152]{1,0:T(8,128)(2,1)S(1)} %get-tuple-element.33), channel_id=1, source_target_pairs={{1,0},{2,1},{3,2},{4,3},{5,4},{6,5},{7,6},{0,7},{9,8},{10,9},{11,1... | collective-permute-start | bytes 442376 | tf_op jit(solution)/shard_map/ppermute | solution.py:235
  42.3 0.1 margin_left.1
  42.4 0.8 collective-permute-start.6
  43.3 1.9 %cross_core.1.cross_ref = f32[4,128,1024]{2,1,0:T(8,128)S(1)} custom-call(bf16[512,1152]{1,0:T(8,128)(2,1)S(1)} %get-tuple-element.31.data_ref, bf16[512,1024]{1,0:T(8,128)(2,1)S(1)} %copy-done.4, bf16[512,640]{1,0:T(8,128)(2,1)S(1)} %copy-done.2, bf16[4,128,512]{2,1,0:T(8,128)(2,1)S(1)} %copy-done.7, bf16[4,1024,128]{2,1,0:T(8,128)(2,1)S(1)} %copy-done), custom_call_target="tpu_custom_call" | custom-call | flops 3000000000 | bytes 6000000 | tf_op jit(solution)/shard_map/cross_core/pallas_call | solution.py:453
  45.2 0.8 collective-permute-done.1.after_ref
  46.0 7.4 %collective-permute-done.before_ref = bf16[64,1152]{1,0:T(8,128)(2,1)S(1)} collective-permute-done((bf16[64,1152]{1,0:T(8,128)(2,1)S(1)}, bf16[64,1152]{1,0:T(8,128)(2,1)S(1)}, u32[]{:S(2)}, u32[]{:S(2)}) %collective-permute-start) | collective-permute-done | bytes 147488 | tf_op jit(solution)/shard_map/ppermute | solution.py:234
  53.4 0.1 margin_data.1
  53.5 0.1 collective-permute-start.4
  53.6 1.2 %collective-permute-start.5 = (bf16[160,1152]{1,0:T(8,128)(2,1)S(1)}, bf16[160,1152]{1,0:T(8,128)(2,1)S(1)}, u32[]{:S(2)}, u32[]{:S(2)}) collective-permute-start(bf16[160,1152]{1,0:T(8,128)(2,1)S(1)} %get-tuple-element.42.token_ref), channel_id=1, source_target_pairs={{8,0},{16,8},{24,16},{32,24},{40,32},{48,40},{56,48},{64,56},{72,6... | collective-permute-start | bytes 1105928 | tf_op jit(solution)/shard_map/ppermute | solution.py:235
  54.8 5.3 %inverse_first.1 = (bf16[4,128,448]{2,1,0:T(8,128)(2,1)S(1)}, bf16[448,1024]{1,0:T(8,128)(2,1)S(1)}, bf16[4,448,1024]{2,1,0:T(8,128)(2,1)S(1)}, f32[4,128,128]{2,1,0:T(8,128)S(1)}) custom-call(f32[4,128,128]{2,1,0:T(8,128)S(1)} %copy-done.9, bf16[64,640]{1,0:T(8,128)(2,1)S(1)} %collective-permute-done.2.before_ref, ...), custom_call_target="tpu_custom_call" | custom-call | flops 4000000000 | bytes 4000000 | tf_op jit(solution)/shard_map/inverse_first/pallas_call | solution.py:403
  60.1 4.0 %inverse_second.1.inv_ref = f32[4,128,128]{2,1,0:T(8,128)S(1)} custom-call(f32[4,128,128]{2,1,0:T(8,128)S(1)} %get-tuple-element.50.part_ref, bf16[160,1152]{1,0:T(8,128)(2,1)S(1)} %get-tuple-element.42.token_ref), custom_call_target="tpu_custom_call" | custom-call | flops 4000000000 | bytes 1000000 | tf_op jit(solution)/shard_map/inverse_second/pallas_call | solution.py:424
  64.0 4.6 %update_residual.1 = (bf16[1024,512]{1,0:T(8,128)(2,1)}, f32[4,128,1024]{2,1,0:T(8,128)S(1)}) custom-call(bf16[512,1152]{1,0:T(8,128)(2,1)S(1)} %get-tuple-element.31.data_ref, bf16[64,1152]{1,0:T(8,128)(2,1)S(1)} %collective-permute-done.before_ref, bf16[64,1152]{1,0:T(8,128)(2,1)S(1)} %collective-permute-done.1.after_ref, ...), custom_call_target="tpu_custom_call" | custom-call | flops 4000000000 | bytes 10000000 | tf_op jit(solution)/shard_map/update_residual/pallas_call | solution.py:502
  68.7 7.1 %all-to-all-start.1 = ((bf16[128,8,512]{2,1,0:T(8,128)(2,1)}), bf16[128,8,512]{2,1,0:T(8,128)(2,1)S(1)}, u32[]{:S(2)}, u32[]{:S(2)}) async-start(bf16[128,8,512]{2,1,0:T(8,128)(2,1)} %bitcast.16), calls=%async_computation.1 | async-start | bytes 2097152 | tf_op jit(solution)/shard_map/all_to_all | solution.py:562
  75.7 2.2 %new_right.1 = f32[4,1024,128]{2,1,0:T(8,128)} custom-call(f32[4,128,1024]{2,1,0:T(8,128)S(1)} %get-tuple-element.51.new_ref), custom_call_target="tpu_custom_call" | custom-call | flops 1000000 | bytes 4000000 | tf_op jit(solution)/shard_map/new_right/pallas_call | solution.py:522
  78.0 15.9 %all-to-all-done.1 = bf16[128,8,512]{2,1,0:T(8,128)(2,1)S(1)} async-done(((bf16[128,8,512]{2,1,0:T(8,128)(2,1)}), bf16[128,8,512]{2,1,0:T(8,128)(2,1)S(1)}, u32[]{:S(2)}, u32[]{:S(2)}) %all-to-all-start.1) | async-done | bytes 1048608 | tf_op jit(solution)/shard_map/all_to_all | solution.py:562
  93.9 1.7 %give_back.1 = bf16[512,1024]{1,0:T(8,128)(2,1)} custom-call(bf16[1024,512]{1,0:T(8,128)(2,1)S(1)} %bitcast.14, s32[512,128]{1,0:T(8,128)S(1)} %copy-done.5), custom_call_target="tpu_custom_call" | custom-call | flops 1000000000 | bytes 4000000 | tf_op jit(solution)/shard_map/give_back/pallas_call | solution.py:549
  (26 shorter events, 0.1 us)
Async XLA Ops:
  4.3 11.5 %copy-start.11 = (s32[512,64]{0,1:T(8,128)S(1)}, s32[512,64]{0,1:T(8,128)}, u32[]{:S(2)}) copy-start(s32[512,64]{0,1:T(8,128)} %param.11) | copy-start | bytes 393220
  4.3 11.7 %copy-start.10 = (bf16[512,4,128]{2,1,0:T(4,128)(2,1)S(1)}, bf16[512,4,128]{2,1,0:T(4,128)(2,1)}, u32[]{:S(2)}) copy-start(bf16[512,4,128]{2,1,0:T(4,128)(2,1)} %param.12) | copy-start | bytes 1572868
  4.4 32.5 %all-to-all-start = ((bf16[128,8,640]{2,1,0:T(8,128)(2,1)}), bf16[128,8,640]{2,1,0:T(8,128)(2,1)S(1)}, u32[]{:S(2)}, u32[]{:S(2)}) async-start(bf16[128,8,640]{2,1,0:T(8,128)(2,1)} %bitcast.15), calls=%async_computation | async-start | bytes 2621440 | tf_op jit(solution)/shard_map/all_to_all | solution.py:562
  16.5 20.3 %copy-start.1 = (bf16[512,640]{1,0:T(8,128)(2,1)}, bf16[512,640]{1,0:T(8,128)(2,1)S(1)}, u32[]{:S(2)}) copy-start(bf16[512,640]{1,0:T(8,128)(2,1)S(1)} %get-tuple-element.29.core_ref.l_ref.lc_ref) | copy-start | bytes 1966084
  16.6 25.8 %collective-permute-start.2 = (bf16[64,640]{1,0:T(8,128)(2,1)S(1)}, bf16[64,640]{1,0:T(8,128)(2,1)S(1)}, u32[]{:S(2)}, u32[]{:S(2)}) collective-permute-start(bf16[64,640]{1,0:T(8,128)(2,1)S(1)} %get-tuple-element.36), channel_id=1, source_target_pairs={{0,1},{1,2},{2,3},{3,4},{4,5},{5,6},{6,7},{7,0},{8,9},{9,10},{10,1... | collective-permute-start | bytes 245768 | tf_op jit(solution)/shard_map/ppermute | solution.py:234
  18.0 24.3 %collective-permute-start.3 = (bf16[64,640]{1,0:T(8,128)(2,1)S(1)}, bf16[64,640]{1,0:T(8,128)(2,1)S(1)}, u32[]{:S(2)}, u32[]{:S(2)}) collective-permute-start(bf16[64,640]{1,0:T(8,128)(2,1)S(1)} %get-tuple-element.37), channel_id=1, source_target_pairs={{1,0},{2,1},{3,2},{4,3},{5,4},{6,5},{7,6},{0,7},{9,8},{10,9},{11,1... | collective-permute-start | bytes 245768 | tf_op jit(solution)/shard_map/ppermute | solution.py:235
  22.9 1.0 %copy-start.3 = (bf16[512,1024]{1,0:T(8,128)(2,1)}, bf16[512,1024]{1,0:T(8,128)(2,1)S(1)}, u32[]{:S(2)}) copy-start(bf16[512,1024]{1,0:T(8,128)(2,1)S(1)} %get-tuple-element.43.seen_ref.seen_c_ref) | copy-start | bytes 3145732
  23.9 0.8 copy-start.6
  24.7 0.7 copy-start.8
  36.9 6.4 %copy-start = (bf16[4,1024,128]{2,1,0:T(8,128)(2,1)S(1)}, bf16[4,1024,128]{2,1,0:T(8,128)(2,1)}, u32[]{:S(2)}) copy-start(bf16[4,1024,128]{2,1,0:T(8,128)(2,1)} %v_ref.3) | copy-start | bytes 3145732
  36.9 6.4 %copy-start.2 = (bf16[512,640]{1,0:T(8,128)(2,1)S(1)}, bf16[512,640]{1,0:T(8,128)(2,1)}, u32[]{:S(2)}) copy-start(bf16[512,640]{1,0:T(8,128)(2,1)} %copy-done.1) | copy-start | bytes 1966084
  36.9 6.4 %copy-start.4 = (bf16[512,1024]{1,0:T(8,128)(2,1)S(1)}, bf16[512,1024]{1,0:T(8,128)(2,1)}, u32[]{:S(2)}) copy-start(bf16[512,1024]{1,0:T(8,128)(2,1)} %copy-done.3) | copy-start | bytes 3145732
  36.9 6.4 %copy-start.7 = (bf16[4,128,512]{2,1,0:T(8,128)(2,1)S(1)}, bf16[4,128,512]{2,1,0:T(8,128)(2,1)}, u32[]{:S(2)}) copy-start(bf16[4,128,512]{2,1,0:T(8,128)(2,1)} %copy-done.6) | copy-start | bytes 1572868
  38.4 7.5 %collective-permute-start.1 = (bf16[64,1152]{1,0:T(8,128)(2,1)S(1)}, bf16[64,1152]{1,0:T(8,128)(2,1)S(1)}, u32[]{:S(2)}, u32[]{:S(2)}) collective-permute-start(bf16[64,1152]{1,0:T(8,128)(2,1)S(1)} %get-tuple-element.33), channel_id=1, source_target_pairs={{1,0},{2,1},{3,2},{4,3},{5,4},{6,5},{7,6},{0,7},{9,8},{10,9},{11,1... | collective-permute-start | bytes 442376 | tf_op jit(solution)/shard_map/ppermute | solution.py:235
  42.3 11.1 %collective-permute-start = (bf16[64,1152]{1,0:T(8,128)(2,1)S(1)}, bf16[64,1152]{1,0:T(8,128)(2,1)S(1)}, u32[]{:S(2)}, u32[]{:S(2)}) collective-permute-start(bf16[64,1152]{1,0:T(8,128)(2,1)S(1)} %get-tuple-element.32.token_ref), channel_id=1, source_target_pairs={{0,1},{1,2},{2,3},{3,4},{4,5},{5,6},{6,7},{7,0},{8,9},{9,10},{10,1... | collective-permute-start | bytes 442376 | tf_op jit(solution)/shard_map/ppermute | solution.py:234
  42.4 12.4 %collective-permute-start.6 = (bf16[160,640]{1,0:T(8,128)(2,1)S(1)}, bf16[160,640]{1,0:T(8,128)(2,1)S(1)}, u32[]{:S(2)}, u32[]{:S(2)}) collective-permute-start(bf16[160,640]{1,0:T(8,128)(2,1)S(1)} %get-tuple-element.45), channel_id=1, source_target_pairs={{0,8},{8,16},{16,24},{24,32},{32,40},{40,48},{48,56},{56,64},{64,7... | collective-permute-start | bytes 614408 | tf_op jit(solution)/shard_map/ppermute | solution.py:234
  43.3 11.5 %collective-permute-start.7 = (bf16[160,640]{1,0:T(8,128)(2,1)S(1)}, bf16[160,640]{1,0:T(8,128)(2,1)S(1)}, u32[]{:S(2)}, u32[]{:S(2)}) collective-permute-start(bf16[160,640]{1,0:T(8,128)(2,1)S(1)} %get-tuple-element.40.token_ref), channel_id=1, source_target_pairs={{8,0},{16,8},{24,16},{32,24},{40,32},{48,40},{56,48},{64,56},{72,6... | collective-permute-start | bytes 614408 | tf_op jit(solution)/shard_map/ppermute | solution.py:235
  43.3 11.5 %copy-start.9 = (f32[4,128,128]{2,1,0:T(8,128)S(1)}, f32[4,128,128]{2,1,0:T(8,128)}, u32[]{:S(2)}) copy-start(f32[4,128,128]{2,1,0:T(8,128)} %copy-done.8) | copy-start | bytes 786436
  53.5 10.6 %collective-permute-start.4 = (bf16[160,1152]{1,0:T(8,128)(2,1)S(1)}, bf16[160,1152]{1,0:T(8,128)(2,1)S(1)}, u32[]{:S(2)}, u32[]{:S(2)}) collective-permute-start(bf16[160,1152]{1,0:T(8,128)(2,1)S(1)} %get-tuple-element.41), channel_id=1, source_target_pairs={{0,8},{8,16},{16,24},{24,32},{32,40},{40,48},{48,56},{56,64},{64,7... | collective-permute-start | bytes 1105928 | tf_op jit(solution)/shard_map/ppermute | solution.py:234
  53.6 10.5 %collective-permute-start.5 = (bf16[160,1152]{1,0:T(8,128)(2,1)S(1)}, bf16[160,1152]{1,0:T(8,128)(2,1)S(1)}, u32[]{:S(2)}, u32[]{:S(2)}) collective-permute-start(bf16[160,1152]{1,0:T(8,128)(2,1)S(1)} %get-tuple-element.42.token_ref), channel_id=1, source_target_pairs={{8,0},{16,8},{24,16},{32,24},{40,32},{48,40},{56,48},{64,56},{72,6... | collective-permute-start | bytes 1105928 | tf_op jit(solution)/shard_map/ppermute | solution.py:235
  68.7 25.2 %all-to-all-start.1 = ((bf16[128,8,512]{2,1,0:T(8,128)(2,1)}), bf16[128,8,512]{2,1,0:T(8,128)(2,1)S(1)}, u32[]{:S(2)}, u32[]{:S(2)}) async-start(bf16[128,8,512]{2,1,0:T(8,128)(2,1)} %bitcast.16), calls=%async_computation.1 | async-start | bytes 2097152 | tf_op jit(solution)/shard_map/all_to_all | solution.py:562
  75.7 18.1 %copy-start.5 = (s32[512,128]{1,0:T(8,128)S(1)}, s32[512,128]{1,0:T(8,128)}, u32[]{:S(2)}) copy-start(s32[512,128]{1,0:T(8,128)} %get-tuple-element.53.place_ref) | copy-start | bytes 786436
